TPU v7x, 32 devices: a whole 2x2x4 slice. The times are simulated.
32 devices in a mesh: seq: 16 (over z, y, x), tp: 2 (over core).
Axes of the slice: x: 2, y: 2, z: 4, core: 2. Of those that a mesh axis runs over, the one named last changes fastest.
Arguments:
- teacher_rows: bfloat16 [7680, 8192], P('seq', 'tp'), may hold values from -2700 to 2700, as said below
- teacher_gain: float32 [8192], P('tp'), may hold values from 0.1 to 1.9
- teacher_counts: int32 [16], replicated, may hold values from 288 to 480, as said below
- projector: bfloat16 [8192, 4096], P('tp', 'seq'), may hold values from -0.0625 to 0.0625
- student_rows: bfloat16 [6144, 4096], P('seq', 'tp'), may hold values from -2700 to 2700
- student_gain: float32 [4096], P('tp'), may hold values from 0.1 to 1.9
- span_shift: int32 [48], P('seq'), may hold values from -128 to 128, as said below
- span_len: int32 [48], P('seq'), may hold values from 64 to 128
- align_weights: bfloat16 [6144, 128], P('seq'), may hold values from 0.0099487305 to 1
Outputs:
- row_grad: bfloat16 [6144, 4096], P('seq', 'tp')
- gain_grad: float32 [4096], P('tp')
Inputs may be any that keep to these rules, and one draw needn't show every extreme that they name: `teacher_counts`: the counts of indices 2m and 2m + 1 add up to 768; one index holds exactly 480 rows in every draw. `teacher_rows`: slots at or beyond an index's count hold no part of the sequence. `span_shift`: for the first block of each index of seq (k = 0) the shift lies in -128 .. -64; for the last (k = 2) it is 128.
All inputs are finite; a program needn't handle non-finite values.
Results may differ from a plain program's by a relative error of at most 0.014.
Values may be sent and summed in bfloat16 or wider, within the bound.
A program may use at most 128 MiB of HBM per device.

v0:
```python
import jax
import jax.numpy as jnp
from jax import lax
from jax.sharding import PartitionSpec as P

epsilon = 1e-06


def padded_2(block, sides, width):
    for axis, dim in sides:
        count = lax.axis_size(axis)
        forward = [(i, i + 1) for i in range(count - 1)]
        backward = [(target, source) for source, target in forward]
        low = lax.ppermute(
            lax.slice_in_dim(block, block.shape[dim] - width, None, axis=dim), axis, forward
        )
        high = lax.ppermute(lax.slice_in_dim(block, 0, width, axis=dim), axis, backward)
        block = jnp.concatenate([low, block, high], axis=dim)
    return block


def shards(
    teacher_rows,
    teacher_gain,
    teacher_counts,
    projector,
    student_rows,
    student_gain,
    span_shift,
    span_len,
    align_weights,
):
    seq_count = lax.axis_size("seq")
    position = lax.axis_index("seq")
    teacher_width = teacher_rows.shape[1] * lax.axis_size("tp")
    student_width = student_rows.shape[1] * lax.axis_size("tp")
    capacity = teacher_rows.shape[0]
    rows_here = student_rows.shape[0]
    block_size = align_weights.shape[1]
    blocks = span_shift.shape[0]
    seq_rows = rows_here * seq_count
    starts = jnp.cumsum(teacher_counts) - teacher_counts
    own_start = jnp.take(starts, position)
    own_count = jnp.take(teacher_counts, position)
    teacher_float = teacher_rows.astype(jnp.float32)
    square_sums = lax.psum(jnp.sum(teacher_float * teacher_float, axis=1), "tp")
    teacher_scale = lax.rsqrt(square_sums / teacher_width + epsilon)
    teacher_normed = (teacher_float * teacher_scale[:, None] * teacher_gain[None, :]).astype(
        jnp.bfloat16
    )
    partials = jnp.dot(
        teacher_normed,
        lax.all_gather(projector, "seq", axis=1, tiled=True),
        preferred_element_type=jnp.float32,
    )
    mapped = lax.psum_scatter(partials.astype(jnp.bfloat16), "tp", scatter_dimension=1, tiled=True)
    halo_width = mapped.shape[0]
    padded = padded_2(mapped, (("seq", 0),), halo_width)
    block_ids = jnp.arange(blocks, dtype=jnp.int32)
    span_start = own_start + block_ids * own_count // blocks + span_shift
    span_start = jnp.clip(span_start, 0, seq_rows - span_len)
    offsets = jnp.arange(block_size, dtype=jnp.int32)
    global_index = span_start[:, None] + offsets[None, :]
    previous_start = jnp.take(starts, jnp.maximum(position - 1, 0))
    next_start = own_start + own_count
    slot_index = jnp.where(
        global_index < own_start,
        global_index - previous_start,
        jnp.where(
            global_index < next_start,
            capacity + global_index - own_start,
            2 * capacity + global_index - next_start,
        ),
    )
    slot_index = jnp.clip(slot_index, 0, 3 * halo_width - 1)
    windows = jnp.take(padded, slot_index.reshape(-1), axis=0).reshape(
        blocks, block_size, mapped.shape[1]
    )
    live_mask = offsets[None, :] < span_len[:, None]
    weights = align_weights.reshape(blocks, block_size, block_size)
    weights = jnp.where(live_mask[:, None, :], weights, jnp.zeros_like(weights))
    target = jnp.einsum(
        "bij,bjc->bic", weights, windows, preferred_element_type=jnp.float32
    ).reshape(rows_here, mapped.shape[1])
    student = student_rows.astype(jnp.float32)
    target_sums, student_sums = lax.psum(
        (jnp.sum(target * target, axis=1), jnp.sum(student * student, axis=1)), "tp"
    )
    target_hat = target * lax.rsqrt(target_sums / student_width + epsilon)[:, None]
    student_scale = lax.rsqrt(student_sums / student_width + epsilon)[:, None]
    student_hat = student * student_scale
    residual = student_hat * student_gain[None, :] - target_hat
    weighted = residual * student_gain[None, :]
    inner_sums = lax.psum(jnp.sum(weighted * student_hat, axis=1), "tp")
    inner_mean = (inner_sums / student_width)[:, None]
    row_grad = (student_scale * (weighted - student_hat * inner_mean)).astype(jnp.bfloat16)
    gain_terms = jnp.sum(residual * student_hat, axis=0)
    gain_grad = lax.psum(gain_terms, "seq") / seq_rows
    return (row_grad, gain_grad)


def solution(mesh):
    placed = (
        P("seq", "tp"),
        P("tp"),
        P(),
        P("tp", "seq"),
        P("seq", "tp"),
        P("tp"),
        P("seq"),
        P("seq"),
        P("seq", None),
    )
    return jax.shard_map(
        shards, mesh=mesh, in_specs=placed, out_specs=(P("seq", "tp"), P("tp")), check_vma=False
    )
```

profile of v0, /device:TPU:0, one launch (start us, length us, event | category | flops | bytes accessed | tf_op | source)
XLA Modules:
  0.0 901.3 jit_solution(6623925578876901047)
XLA Ops:
  7.2 0.0 copy-start.4
  7.2 0.0 all-gather.2.cloned.1.call-start
  7.2 0.7 all-gather.2.cloned.1.call-update
  7.9 0.0 reduce-scatter.2.cloned.1.call-start
  8.0 3.0 fusion
  10.9 2.6 psum.36
  13.5 682.7 %all-gather.2.cloned.1.call-done = bf16[4096,4096]{1,0:T(8,128)(2,1)} async-done(((bf16[4096,256]{1,0:T(8,128)(2,1)}), bf16[4096,4096]{1,0:T(8,128)(2,1)}) %all-gather.2.cloned.1.call-update) | async-done | bytes 33554448 | tf_op jit(solution)/shard_map/all_gather | solution.py:53
  696.2 0.0 copy-done.4
  696.2 24.9 %convolution_convert_fusion = bf16[480,4096]{1,0:T(8,128)(2,1)} fusion(bf16[4096,4096]{1,0:T(8,128)(2,1)} %all-gather.2.cloned.1.call-done, bf16[480,4096]{1,0:T(8,128)(2,1)} %param.9, f32[4096]{0:T(1024)S(1)} %copy-done.4, f32[480]{0:T(512)S(1)} %add_rsqrt_fusion.1), kind=kOutput, calls=%fused_computation.7 | convolution fusion | flops 16115957760 | bytes 41437056 | tf_op jit(solution)/shard_map/dot_general | solution.py:51
  721.1 0.0 copy-start.3
  721.1 0.0 copy-start
  721.1 0.0 reduce-scatter.2.cloned.1.call-update
  721.1 13.2 %reduce-scatter.2.cloned.1.call-done = bf16[480,2048]{1,0:T(8,128)(2,1)} async-done(((bf16[480,4096]{1,0:T(8,128)(2,1)}), bf16[480,2048]{1,0:T(8,128)(2,1)}) %reduce-scatter.2.cloned.1.call-update) | async-done | bytes 1966096 | tf_op jit(solution)/shard_map/reduce_scatter | solution.py:56
  734.4 1.3 collective-permute-start.1
  735.6 5.9 collective-permute-start
  741.6 0.0 copy-done.3
  741.6 0.6 dynamic-slice.7
  742.2 0.1 copy.12
  742.3 0.1 reduce.1
  742.4 0.7 sub.72
  743.1 0.7 fusion.30
  745.6 0.7 maximum_minimum_fusion
  746.3 0.1 fusion.27
  746.5 0.0 copy-done
  746.5 0.4 fusion.16
  746.8 0.7 iota_compare_fusion
  747.6 34.5 %collective-permute-done.1 = bf16[480,2048]{1,0:T(8,128)(2,1)S(1)} collective-permute-done((bf16[480,2048]{1,0:T(8,128)(2,1)}, bf16[480,2048]{1,0:T(8,128)(2,1)S(1)}, u32[]{:S(2)}, u32[]{:S(2)}) %collective-permute-start.1) | collective-permute-done | bytes 1966112 | tf_op jit(solution)/shard_map/ppermute | solution.py:17
  782.1 42.7 %collective-permute-done = bf16[480,2048]{1,0:T(8,128)(2,1)} collective-permute-done((bf16[480,2048]{1,0:T(8,128)(2,1)}, bf16[480,2048]{1,0:T(8,128)(2,1)}, u32[]{:S(2)}, u32[]{:S(2)}) %collective-permute-start) | collective-permute-done | bytes 1966112 | tf_op jit(solution)/shard_map/ppermute | solution.py:14
  824.8 5.6 pad_maximum_fusion
  830.4 0.0 copy-start.1
  830.4 8.5 gather_fusion
  838.9 0.0 copy-start.2
  838.9 0.0 copy-done.1
  838.9 2.1 multiply_reduce_fusion
  841.1 2.6 all-reduce
  843.7 0.0 copy-done.2
  843.7 2.6 fusion.15
  846.4 2.5 psum.38
  848.8 3.6 fusion.14
  852.5 41.4 %psum.39 = f32[2048]{0:T(1024)S(1)} all-reduce(f32[2048]{0:T(1024)S(1)} %get-tuple-element.35), channel_id=1, replica_groups=mesh['seq'=16,'tp'=2] {'seq'}, use_global_device_ids=true, to_apply=%region_11.12 | all-reduce | flops 2048 | bytes 16384 | tf_op jit(solution)/shard_map/psum | solution.py:98
  893.8 0.6 broadcast_multiply_fusion
  (7 shorter events, 0.1 us)
Async XLA Ops:
  7.2 689.0 %copy-start.4 = (f32[4096]{0:T(1024)S(1)}, f32[4096]{0:T(1024)}, u32[]{:S(2)}) copy-start(f32[4096]{0:T(1024)} %param.10) | copy-start | bytes 49156
  7.2 689.0 %all-gather.2.cloned.1.call-start = ((), (), s32[]{:S(2)}) async-start(), calls=%async_computation.1 | async-start | bytes 35651584 | tf_op jit(solution)/shard_map/all_gather | solution.py:53
  7.9 726.5 %reduce-scatter.2.cloned.1.call-start = ((), (), s32[]{:S(2)}) async-start(), calls=%async_computation.2 | async-start | bytes 5898240 | tf_op jit(solution)/shard_map/reduce_scatter | solution.py:56
  721.1 20.5 %copy-start.3 = (s32[16]{0:T(128)S(1)}, s32[16]{0:T(128)}, u32[]{:S(2)}) copy-start(s32[16]{0:T(128)} %param.11) | copy-start | bytes 196
  721.1 25.4 %copy-start = (bf16[384,2048]{1,0:T(8,128)(2,1)S(1)}, bf16[384,2048]{1,0:T(8,128)(2,1)}, u32[]{:S(2)}) copy-start(bf16[384,2048]{1,0:T(8,128)(2,1)} %param.13) | copy-start | bytes 4718596
  734.4 47.7 %collective-permute-start.1 = (bf16[480,2048]{1,0:T(8,128)(2,1)}, bf16[480,2048]{1,0:T(8,128)(2,1)S(1)}, u32[]{:S(2)}, u32[]{:S(2)}) collective-permute-start(bf16[480,2048]{1,0:T(8,128)(2,1)} %reduce-scatter.2.cloned.1.call-done), channel_id=1, source_target_pairs={{2,0},{4,2},{6,4},{8,6},{10,8},{12,10},{14,12},{16,14},{18,16},{20... | collective-permute-start | bytes 5898248 | tf_op jit(solution)/shard_map/ppermute | solution.py:17
  735.6 89.1 %collective-permute-start = (bf16[480,2048]{1,0:T(8,128)(2,1)}, bf16[480,2048]{1,0:T(8,128)(2,1)}, u32[]{:S(2)}, u32[]{:S(2)}) collective-permute-start(bf16[480,2048]{1,0:T(8,128)(2,1)} %reduce-scatter.2.cloned.1.call-done), channel_id=1, source_target_pairs={{0,2},{2,4},{4,6},{6,8},{8,10},{10,12},{12,14},{14,16},{16,18},{18... | collective-permute-start | bytes 5898248 | tf_op jit(solution)/shard_map/ppermute | solution.py:14
  830.4 8.5 copy-start.1
  838.9 4.8 copy-start.2
Sparse Core Ops, SparseCore 0:
  9.5 686.6 all-gather.1
  721.2 13.0 reduce-scatter.1
where the time goes:
time: 902 us; the launch traced here: 901 us
  waiting for transfers between devices  774 us (86%)
  blocking collectives  49.1 us (5%)
  matrix products  27 us (3%)
  other arithmetic  18.2 us (2%)
  between operations  16 us (2%)
  local copies, waits for them, and re-layouts  9.88 us (1%)
    all_gather x1, waiting for transfers between devices, shards(): lax.all_gather(projector, 'seq', axis=1, tiled=True)  683 us
    ppermute x1, waiting for transfers between devices, padded_2(): lax.ppermute(lax.slice_in_dim(block, block.shape[dim] - width, None, axis...  42.7 us
    psum x1, blocking collectives, shards(): gain_grad = lax.psum(gain_terms, 'seq') / seq_rows  41.4 us
    ppermute x1, waiting for transfers between devices, padded_2(): lax.ppermute(lax.slice_in_dim(block, 0, width, axis=dim), axis, backward)  34.5 us
    dot_general x1, matrix products, shards(): jnp.dot(teacher_normed, lax.all_gather(projector, 'seq', axis=1, tiled=Tr...  24.9 us
  transfers between devices with their start and end apart: 4, of which 4 were waited for; matrix products, arithmetic and copies ran while one was open for 1% of the time, Pallas kernels for 0%

commit v1 on v0

v1 whole, which is shorter than its diff:
```python
import functools

import jax
import jax.numpy as jnp
from jax import lax
from jax.experimental import pallas as pl
from jax.experimental.pallas import tpu as pltpu
from jax.sharding import PartitionSpec as P

epsilon = 1e-06
MESH = pl.DeviceIdType.MESH
VMEM_LIMIT = 52 * 1024 * 1024


def group_size(count):
    size = 1
    while size * size < count:
        size *= 2
    return size


def partner(p, e, g):
    if g == 4:
        if e == 0:
            return p, p
        low, high = 1 - 2 * (p % 2), 2 - 4 * (p // 2)
        other = p + (low if e % 2 else 0) + (high if e // 2 else 0)
        return other, other
    return (p - e + g) % g, (p + e) % g


def gather_kernel(
    g, nq, tp, nh,
    x_hbm, p_hbm, w_hbm, a_hbm,
    mapped, w_all, a_all,
    xs, ps, part, recv,
    x_send, x_recv, u_send, d_send, p_recv, s_send, s_recv, t_send, t_recv, local,
):
    me, t = lax.axis_index("seq"), lax.axis_index("tp")
    p, q = me % g, me // g
    base = q * g
    half = xs.shape[1]
    nl = nq // tp

    barrier = pltpu.get_barrier_semaphore()
    for e in range(1, g):
        pl.semaphore_signal(barrier, inc=1, device_id=(base + (p + e) % g, t), device_id_type=MESH)
    for o in range(1, tp):
        pl.semaphore_signal(barrier, inc=1, device_id=(me, (t + o) % tp), device_id_type=MESH)

    @pl.when(q > 0)
    def _():
        pl.semaphore_signal(barrier, inc=1, device_id=(me - g, t), device_id_type=MESH)

    @pl.when(q < nq - 1)
    def _():
        pl.semaphore_signal(barrier, inc=1, device_id=(me + g, t), device_id_type=MESH)

    ends = (q == 0).astype(jnp.int32) + (q == nq - 1).astype(jnp.int32)
    pl.semaphore_wait(barrier, g - 1 + tp - 1 + 2 - ends)

    def x_copy(source, e, h, member):
        return pltpu.make_async_remote_copy(
            src_ref=source, dst_ref=xs.at[e * nh + h],
            send_sem=x_send.at[e * nh + h], recv_sem=x_recv.at[e * nh + h],
            device_id=(base + member, t), device_id_type=MESH,
        )

    def own(h):
        return x_hbm.at[pl.ds(h * half, half)]

    def p_copy(source, block, sem, seq):
        return pltpu.make_async_remote_copy(
            src_ref=source, dst_ref=ps.at[block], send_sem=sem, recv_sem=p_recv.at[block],
            device_id=(seq, t), device_id_type=MESH,
        )

    relayed = g == 4
    direct = [1, 2] if relayed else list(range(1, g))

    def up(s):
        return p_copy(p_hbm if s == 0 else ps.at[q - s], q - s, u_send.at[s], me + g)

    def down(s):
        return p_copy(p_hbm if s == 0 else ps.at[q + s], q + s, d_send.at[s], me - g)

    def forward(s):
        @pl.when(q - s >= 0)
        def _():
            if s > 0:
                p_copy(p_hbm, q - s, u_send.at[0], me).wait_recv()

            @pl.when(q < nq - 1)
            def _():
                up(s).start()

        @pl.when(q + s < nq)
        def _():
            if s > 0:
                p_copy(p_hbm, q + s, u_send.at[0], me).wait_recv()

            @pl.when(q > 0)
            def _():
                down(s).start()

    first = []
    for h in range(nh):
        for e in direct:
            k = nh - 1 - h if e == 2 else h
            first.append((e, k))
    for e, h in first[: len(direct)]:
        x_copy(own(h), e, h, partner(p, e, g)[1]).start()
    forward(0)
    for e, h in first[len(direct):]:
        x_copy(own(h), e, h, partner(p, e, g)[1]).start()

    smalls = []
    for index, (source, target) in enumerate(((w_hbm, w_all), (a_hbm, a_all))):
        for e in range(1, g):
            copy = pltpu.make_async_remote_copy(
                src_ref=source, dst_ref=target.at[p],
                send_sem=s_send.at[index, e], recv_sem=s_recv.at[index, e],
                device_id=(base + (p + e) % g, t), device_id_type=MESH,
            )
            copy.start()
            smalls.append(copy)
    locals_ = [
        pltpu.make_async_copy(p_hbm, ps.at[q], local.at[0]),
        pltpu.make_async_copy(w_hbm, w_all.at[p], local.at[1]),
        pltpu.make_async_copy(a_hbm, a_all.at[p], local.at[2]),
    ]
    for h in range(nh):
        locals_.append(pltpu.make_async_copy(own(h), xs.at[h], local.at[3 + h]))
    for copy in locals_:
        copy.start()
    for copy in locals_:
        copy.wait()

    def multiply(c0, c1, b0, b1):
        def blocks(b, carry):
            def chunks(c, inner):
                part[b, c] = jnp.dot(
                    xs[c], ps[b], preferred_element_type=jnp.float32
                ).astype(jnp.bfloat16)
                return inner

            return lax.fori_loop(c0, c1, chunks, carry)

        lax.fori_loop(b0, b1, blocks, 0)

    def near(s):
        return jnp.maximum(q - s, 0), jnp.minimum(q + s, nq - 1) + 1

    def at_distance(s, c0, c1):
        @pl.when(q - s >= 0)
        def _():
            multiply(c0, c1, q - s, q - s + 1)

        @pl.when(q + s < nq)
        def _():
            multiply(c0, c1, q + s, q + s + 1)

    for e, h in first[: len(direct)]:
        copy = x_copy(own(h), e, h, partner(p, e, g)[1])
        copy.wait_recv()
        if relayed:
            x_copy(xs.at[e * nh + h], 3, h, partner(p, 3 - e, g)[1]).start()
    forward(1)
    for e, h in first[len(direct):]:
        x_copy(own(h), e, h, partner(p, e, g)[1]).wait_recv()
    early = (1 + len(direct)) * nh
    multiply(0, early, *near(1))
    for s in range(2, nq - 1):
        forward(s)
        at_distance(s, 0, early)
    if relayed:
        for h in range(nh):
            x_copy(xs.at[3 * nh + h], 3, h, p).wait_recv()
        multiply(early, g * nh, *near(nq - 2))
    forward(nq - 1)
    at_distance(nq - 1, 0, g * nh)

    sums = []
    for o in range(1, tp):
        other = (t + o) % tp
        copy = pltpu.make_async_remote_copy(
            src_ref=part.at[pl.ds(other * nl, nl)], dst_ref=recv.at[o - 1],
            send_sem=t_send.at[o - 1], recv_sem=t_recv.at[o - 1],
            device_id=(me, other), device_id_type=MESH,
        )
        copy.start()
        sums.append(copy)
    for copy in smalls + sums:
        copy.wait()

    def add(i, carry):
        block, chunk = i // (g * nh), i % (g * nh)
        total = part[t * nl + block, chunk].astype(jnp.float32)
        for o in range(1, tp):
            total += recv[o - 1, block, chunk].astype(jnp.float32)
        mapped[block, chunk] = total.astype(jnp.bfloat16)
        return carry

    lax.fori_loop(0, nl * g * nh, add, 0)

    for e, h in first:
        x_copy(own(h), e, h, partner(p, e, g)[1]).wait_send()
    if relayed:
        for e, h in first[: len(direct)]:
            x_copy(xs.at[e * nh + h], 3, h, partner(p, 3 - e, g)[1]).wait_send()
    for s in range(nq - 1):
        @pl.when((q - s >= 0) & (q < nq - 1))
        def _():
            up(s).wait_send()

        @pl.when((q + s < nq) & (q > 0))
        def _():
            down(s).wait_send()


def gather_map(g, nq, tp, x, p, w, a):
    rows, depth = x.shape
    width = p.shape[1]
    nh = 2 if rows % 32 == 0 else 1
    half = rows // nh
    nl = nq // tp
    any_spec = pl.BlockSpec(memory_space=pl.ANY)
    vmem = pl.BlockSpec(memory_space=pltpu.VMEM)
    dma = pltpu.SemaphoreType.DMA
    return pl.pallas_call(
        functools.partial(gather_kernel, g, nq, tp, nh),
        out_shape=(
            jax.ShapeDtypeStruct((nl, g * nh, half, width), jnp.bfloat16),
            jax.ShapeDtypeStruct((g,) + w.shape, w.dtype),
            jax.ShapeDtypeStruct((g,) + a.shape, a.dtype),
        ),
        in_specs=[any_spec] * 4,
        out_specs=(vmem, vmem, vmem),
        scratch_shapes=[
            pltpu.VMEM((g * nh, half, depth), jnp.bfloat16),
            pltpu.VMEM((nq, depth, width), jnp.bfloat16),
            pltpu.VMEM((nq, g * nh, half, width), jnp.bfloat16),
            pltpu.VMEM((max(tp - 1, 1), nl, g * nh, half, width), jnp.bfloat16),
            dma((g * nh,)),
            dma((g * nh,)),
            dma((nq,)),
            dma((nq,)),
            dma((nq,)),
            dma((2, g)),
            dma((2, g)),
            dma((tp,)),
            dma((tp,)),
            dma((3 + nh,)),
        ],
        compiler_params=pltpu.CompilerParams(
            collective_id=0, has_side_effects=True, vmem_limit_bytes=VMEM_LIMIT
        ),
        cost_estimate=pl.CostEstimate(
            flops=2 * g * rows * depth * nq * width,
            bytes_accessed=2 * (g * rows * depth + nq * depth * width),
            transcendentals=0,
        ),
    )(x, p, w, a)


def sum_kernel(n, value, total, held, send_sem, recv_sem):
    me, t = lax.axis_index("seq"), lax.axis_index("tp")
    barrier = pltpu.get_barrier_semaphore()
    for o in range(1, n):
        pl.semaphore_signal(barrier, inc=1, device_id=((me + o) % n, t), device_id_type=MESH)
    pl.semaphore_wait(barrier, n - 1)
    copies = []
    for o in range(1, n):
        copy = pltpu.make_async_remote_copy(
            src_ref=value, dst_ref=held.at[o],
            send_sem=send_sem.at[o], recv_sem=recv_sem.at[o],
            device_id=((me + o) % n, t), device_id_type=MESH,
        )
        copy.start()
        copies.append(copy)
    acc = value[...]
    for o, copy in zip(range(1, n), copies):
        copy.wait_recv()
        acc += held[o]
    total[...] = acc
    for copy in copies:
        copy.wait_send()


def sum_over_seq(n, value):
    vmem = pl.BlockSpec(memory_space=pltpu.VMEM)
    dma = pltpu.SemaphoreType.DMA
    return pl.pallas_call(
        functools.partial(sum_kernel, n),
        out_shape=jax.ShapeDtypeStruct(value.shape, value.dtype),
        in_specs=[vmem],
        out_specs=vmem,
        scratch_shapes=[pltpu.VMEM((n,) + value.shape, value.dtype), dma((n,)), dma((n,))],
        compiler_params=pltpu.CompilerParams(collective_id=1, has_side_effects=True),
    )(value)


def shards(
    teacher_rows,
    teacher_gain,
    teacher_counts,
    projector,
    student_rows,
    student_gain,
    span_shift,
    span_len,
    align_weights,
):
    n, tp = lax.axis_size("seq"), lax.axis_size("tp")
    me = lax.axis_index("seq")
    g = group_size(n)
    nq = n // g
    p, q = me % g, me // g
    teacher_width = teacher_rows.shape[1] * tp
    student_width = student_rows.shape[1] * tp
    capacity = teacher_rows.shape[0]
    rows_here = student_rows.shape[0]
    block_size = align_weights.shape[1]
    blocks = span_shift.shape[0]
    width = projector.shape[1]
    nl = nq // tp
    seq_rows = rows_here * n

    teacher_float = teacher_rows.astype(jnp.float32)
    squares = jnp.sum(teacher_float * teacher_float, axis=1)
    aux = jnp.concatenate(
        [squares, span_shift.astype(jnp.float32), span_len.astype(jnp.float32)]
    )
    aux_rows = -(-aux.shape[0] // 1024) * 8
    aux = jnp.pad(aux, (0, aux_rows * 128 - aux.shape[0])).reshape(aux_rows, 128)
    scaled = (projector.astype(jnp.float32) * teacher_gain[:, None]).astype(jnp.bfloat16)
    mapped, weights, aux_all = gather_map(g, nq, tp, teacher_rows, scaled, align_weights, aux)
    aux_all = aux_all.reshape(g, aux_rows * 128)
    square_sums = lax.psum(aux_all[:, :capacity], "tp")
    scales = lax.rsqrt(square_sums / teacher_width + epsilon)
    shifts = aux_all[:, capacity : capacity + blocks].astype(jnp.int32)
    lengths = aux_all[:, capacity + blocks : capacity + 2 * blocks].astype(jnp.int32)

    members = jnp.arange(g, dtype=jnp.int32)
    if g == 4:
        slot_of = jnp.bitwise_xor(members, p)
    else:
        slot_of = (p - members + g) % g
    mapped = mapped.reshape(nl, g, capacity, width)
    scale_slots = jnp.take(scales, slot_of, axis=0)
    mapped = (mapped.astype(jnp.float32) * scale_slots[None, :, :, None]).astype(jnp.bfloat16)

    starts = jnp.cumsum(teacher_counts) - teacher_counts
    low = block_size
    high = 2 * block_size - (2 * rows_here - capacity) // blocks
    last_count = jnp.take(teacher_counts, q * g + g - 1)
    tail = lax.dynamic_slice(
        mapped, (0, slot_of[g - 1], last_count - low, 0), (nl, 1, low, width)
    )[:, 0]
    head = lax.dynamic_slice(mapped, (0, slot_of[0], 0, 0), (nl, 1, high, width))[:, 0]
    below = lax.ppermute(tail, "seq", [(i, i + g) for i in range(n - g)])
    above = lax.ppermute(head, "seq", [(i + g, i) for i in range(n - g)])
    padded = jnp.concatenate([below, mapped.reshape(nl, g * capacity, width), above], axis=1)

    ids = q * g + members
    counts = jnp.take(teacher_counts, ids)
    own = jnp.take(starts, ids)
    block_ids = jnp.arange(blocks, dtype=jnp.int32)
    span = own[:, None] + block_ids[None, :] * counts[:, None] // blocks + shifts
    span = jnp.clip(span, 0, seq_rows - lengths)
    offsets = jnp.arange(block_size, dtype=jnp.int32)
    index = span[:, :, None] + offsets
    before = jnp.take(starts, jnp.maximum(ids - 1, 0))
    slot_before = jnp.take(slot_of, jnp.maximum(members - 1, 0))
    slot_after = jnp.take(slot_of, jnp.minimum(members + 1, g - 1))
    base_before = jnp.where(members == 0, low - own, low + slot_before * capacity - before)
    base_own = low + slot_of * capacity - own
    base_after = jnp.where(members == g - 1, low + g * capacity, low + slot_after * capacity) - (
        own + counts
    )
    wide = lambda v: v[:, None, None]
    slot = index + jnp.where(
        index < wide(own),
        wide(base_before),
        jnp.where(index < wide(own + counts), wide(base_own), wide(base_after)),
    )
    slot = jnp.clip(slot, 0, padded.shape[1] - 1)
    windows = jnp.take(padded, slot.reshape(-1), axis=1).reshape(
        nl, g * blocks, block_size, width
    )
    live = (offsets < lengths[:, :, None]).reshape(g * blocks, 1, block_size)
    weights = weights.reshape(g * blocks, block_size, block_size)
    weights = jnp.where(live, weights, jnp.zeros_like(weights))
    mixed = jnp.einsum("bij,zbjc->bizc", weights, windows, preferred_element_type=jnp.float32)
    mixed = mixed.astype(jnp.bfloat16).reshape(g, rows_here, nl, width)

    pieces = []
    for e in range(g):
        piece = lax.dynamic_index_in_dim(mixed, partner(p, e, g)[1], 0, keepdims=False)
        if e:
            hops = [(i, i // g * g + partner(i % g, e, g)[1]) for i in range(n)]
            piece = lax.ppermute(piece, "seq", hops)
        pieces.append(piece)
    target = jnp.take(jnp.stack(pieces), slot_of, axis=0)
    target = jnp.transpose(target, (1, 2, 0, 3)).reshape(rows_here, nl * g * width)
    target = target.astype(jnp.float32)

    student = student_rows.astype(jnp.float32)
    target_sums, student_sums = lax.psum(
        (jnp.sum(target * target, axis=1), jnp.sum(student * student, axis=1)), "tp"
    )
    target_hat = target * lax.rsqrt(target_sums / student_width + epsilon)[:, None]
    student_scale = lax.rsqrt(student_sums / student_width + epsilon)[:, None]
    student_hat = student * student_scale
    residual = student_hat * student_gain[None, :] - target_hat
    weighted = residual * student_gain[None, :]
    inner_sums = lax.psum(jnp.sum(weighted * student_hat, axis=1), "tp")
    inner_mean = (inner_sums / student_width)[:, None]
    row_grad = (student_scale * (weighted - student_hat * inner_mean)).astype(jnp.bfloat16)
    gain_terms = jnp.sum(residual * student_hat, axis=0)
    gain_grad = sum_over_seq(n, gain_terms.reshape(-1, 128)).reshape(-1) / seq_rows
    return (row_grad, gain_grad)


def solution(mesh):
    placed = (
        P("seq", "tp"),
        P("tp"),
        P(),
        P("tp", "seq"),
        P("seq", "tp"),
        P("tp"),
        P("seq"),
        P("seq"),
        P("seq", None),
    )
    return jax.shard_map(
        shards, mesh=mesh, in_specs=placed, out_specs=(P("seq", "tp"), P("tp")), check_vma=False
    )
```

time: 902 us -> 273 us (0.30)
  waiting for transfers between devices: 774 us -> 16.6 us
  Pallas kernels: 0 us -> 171 us
  blocking collectives: 49.1 us -> 7.45 us
  local copies, waits for them, and re-layouts: 9.88 us -> 37.8 us
  matrix products: 27 us -> 0.65 us
  between operations: 16 us -> 5.55 us
  other arithmetic: 18.2 us -> 27.7 us
    all_gather x1 -> x0, waiting for transfers between devices: 683 us -> none  [shards(): lax.all_gather(projector, 'seq', axis=1, tiled=True)]
    pallas_call x0 -> x2, Pallas kernels: none -> 171 us  [the longest x1 159 us: gather_map(): pl.pallas_call(functools.partial(gather_kernel, g, nq, tp, nh), out_shape...]
    ppermute x2 -> x5, waiting for transfers between devices: 77.2 us -> 16.6 us  [the longest x3 16.5 us: shards(): piece = lax.ppermute(piece, 'seq', hops)]
    psum x2 -> x1, blocking collectives: 44 us -> 2.54 us  [shards(): square_sums = lax.psum(aux_all[:, :capacity], 'tp')]
    dot_general x2 -> x1, matrix products: 27 us -> 0.65 us  [shards(): jnp.einsum('bij,zbjc->bizc', weights, windows, preferred_element_type=jnp...]
    concatenate x0 -> x1, local copies, waits for them, and re-layouts: none -> 13.9 us  [shards(): jnp.concatenate([below, mapped.reshape(nl, g * capacity, width), above],...]
    reduce_scatter x1 -> x0, waiting for transfers between devices: 13.2 us -> none  [shards(): lax.psum_scatter(partials.astype(jnp.bfloat16), 'tp', scatter_dimension=1...]
    convert_element_type x0 -> x8, other arithmetic: none -> 12 us  [the longest x2 4.43 us: shards(): (mapped.astype(jnp.float32) * scale_slots[None, :, :, None]).astype(jnp.b...]
  transfers between devices with their start and end apart: 4 -> 5, of which waited for: 4 -> 2; matrix products, arithmetic and copies ran while one was open for 1% -> 3% of each run, Pallas kernels for 0% -> 0%
where the time goes in v1:
time: 273 us
  Pallas kernels  171 us (63%)
  local copies, waits for them, and re-layouts  37.8 us (14%)
  other arithmetic  27.7 us (10%)
  waiting for transfers between devices  16.6 us (6%)
  blocking collectives  7.45 us (3%)
  starting transfers between devices  6.26 us (2%)
  between operations  5.55 us (2%)
    pallas_call x1, Pallas kernels, gather_map(): pl.pallas_call(functools.partial(gather_kernel, g, nq, tp, nh), out_shape...  159 us
    ppermute x3, waiting for transfers between devices, shards(): piece = lax.ppermute(piece, 'seq', hops)  16.5 us
    concatenate x1, local copies, waits for them, and re-layouts, shards(): jnp.concatenate([below, mapped.reshape(nl, g * capacity, width), above],...  13.9 us
    pallas_call x1, Pallas kernels, sum_over_seq(): pl.pallas_call(functools.partial(sum_kernel, n), out_shape=jax.ShapeDtype...  11.4 us
    gather x2, local copies, waits for them, and re-layouts, shards(): jnp.take(padded, slot.reshape(-1), axis=1)  8.19 us
  transfers between devices with their start and end apart: 5, of which 2 were waited for; matrix products, arithmetic and copies ran while one was open for 3% of the time, Pallas kernels for 0%

profile of v1, /device:TPU:0, one launch (start us, length us, event | category | flops | bytes accessed | tf_op | source)
XLA Modules:
  0.0 272.6 jit_solution(11887863362520738644)
XLA Ops:
  0.7 0.6 fusion.33
  2.6 3.0 %multiply_reduce_fusion = f32[480]{0:T(512)S(1)} fusion(bf16[480,4096]{1,0:T(8,128)(2,1)} %x_hbm.1), kind=kLoop, calls=%fused_computation.8 | loop fusion | flops 5897760 | bytes 3934080 | tf_op jit(solution)/shard_map/reduce_sum | solution.py:330
  5.7 1.7 multiply_convert_fusion.p_hbm
  7.5 159.3 %shard_map.104 = (bf16[2,8,240,256]{3,2,1,0:T(8,128)(2,1)}, bf16[4,384,128]{2,1,0:T(8,128)(2,1)S(1)}, f32[4,8,128]{2,1,0:T(8,128)S(1)}) custom-call(bf16[480,4096]{1,0:T(8,128)(2,1)} %x_hbm.1, bf16[4096,256]{1,0:T(8,128)(2,1)} %multiply_convert_fusion.p_hbm, bf16[384,128]{1,0:T(8,128)(2,1)S(1)} %copy-done, f32[8,128]{1,0:T(8,128)S(1)} %fusion.23.a_hbm), custom_call_target="tpu_custom_call" | custom-call | flops 16106127360 | bytes 24117248 | tf_op jit(solution)/shard_map/pallas_call | solution.py:230
  166.8 2.5 psum.29
  169.4 3.8 %convert_element_type.83 = f32[2,8,240,256]{3,2,1,0:T(8,128)} convert(bf16[2,8,240,256]{3,2,1,0:T(8,128)(2,1)} %get-tuple-element.9) | non-fusion elementwise | flops 983040 | bytes 5898240 | tf_op jit(solution)/shard_map/convert_element_type | solution.py:351
  173.2 0.6 dynamic-slice.2
  174.4 0.6 gather_fusion
  175.1 2.4 fusion.1
  178.2 1.3 collective-permute-start
  181.5 1.5 collective-permute-start.1
  183.1 0.6 gather_fusion.7
  183.8 0.1 reduce.2
  184.0 0.6 gather_fusion.4
  184.6 0.6 gather_fusion.3
  185.6 2.0 fusion
  187.6 0.6 gather_fusion.5
  188.2 0.6 gather_fusion.6
  189.4 0.1 broadcast_in_dim.126
  189.6 0.1 broadcast_in_dim.129
  190.1 0.1 lt.169
  190.3 0.1 compare_and_fusion
  190.5 0.1 pad_maximum_fusion
  190.7 13.9 %copy.33 = bf16[2,2208,256]{2,0,1:T(2,128)(2,1)S(1)} copy(bf16[2,2208,256]{2,1,0:T(8,128)(2,1)S(1)} %pad_maximum_fusion) | data formatting | bytes 4521984 | tf_op jit(solution)/shard_map/concatenate | solution.py:363
  204.6 6.6 %gather_fusion.1 = bf16[1536,2,256]{2,1,0:T(2,128)(2,1)} fusion(bf16[2,2208,256]{2,0,1:T(2,128)(2,1)S(1)} %copy.33, s32[2048]{0:T(1024)S(1)} %pad_clamp_fusion), kind=kCustom, calls=%fused_computation.6 | custom fusion | bytes 3151872 | tf_op jit(solution)/shard_map/jit(_take)/gather | solution.py:388
  211.2 1.6 copy.34
  212.8 0.7 convolution_convert_fusion
  213.5 0.1 copy.36
  213.6 1.1 dynamic-slice_bitcast_fusion.3
  214.7 1.5 collective-permute-start.2
  216.2 0.5 collective-permute-start.3
  216.7 1.5 collective-permute-start.4
  218.2 0.9 copy.31
  219.0 0.4 fusion.12
  219.4 7.5 %collective-permute-done.2 = bf16[384,2,256]{2,0,1:T(8,128)(2,1)} collective-permute-done((bf16[384,2,256]{2,0,1:T(8,128)(2,1)}, bf16[384,2,256]{2,0,1:T(8,128)(2,1)}, u32[]{:S(2)}, u32[]{:S(2)}) %collective-permute-start.2) | collective-permute-done | bytes 393248 | tf_op jit(solution)/shard_map/ppermute | solution.py:402
  226.9 9.1 %collective-permute-done.3 = bf16[384,2,256]{2,0,1:T(8,128)(2,1)} collective-permute-done((bf16[384,2,256]{2,0,1:T(8,128)(2,1)}, bf16[384,2,256]{2,0,1:T(8,128)(2,1)}, u32[]{:S(2)}, u32[]{:S(2)}) %collective-permute-start.3) | collective-permute-done | bytes 393248 | tf_op jit(solution)/shard_map/ppermute | solution.py:402
  236.0 2.6 pad_maximum_fusion.1
  238.6 2.1 gather_fusion.2
  240.6 1.9 convert_bitcast_fusion
  242.6 0.6 fusion.13
  243.1 2.4 copy.38
  245.5 2.5 all-reduce.1
  248.0 3.3 %fusion.11 = (f32[2048]{0:T(1024)}, f32[384]{0:T(512)S(1)}) fusion(bf16[384,2048]{0,1:T(8,128)(2,1)} %copy-done.2, f32[384,2,4,256]{0,3,2,1:T(8,128)S(1)} %copy.38, f32[384]{0:T(512)S(1)} %add_rsqrt_fusion.1, f32[2048]{0:T(1024)S(1)} %copy-done.5, f32[384]{0:T(512)S(1)} %add_rsqrt_fusion.2), kind=kLoop, calls=%fused_computation.27 | loop fusion | flops 7861888 | bytes 4739584 | tf_op jit(solution)/shard_map/reduce_sum | solution.py:420
  251.3 2.4 psum.31
  253.8 3.6 %fusion.10 = bf16[384,2048]{0,1:T(8,128)(2,1)} fusion(bf16[384,2048]{0,1:T(8,128)(2,1)} %copy-done.2, f32[384,2,4,256]{0,3,2,1:T(8,128)S(1)} %copy.38, f32[384]{0:T(512)S(1)} %broadcast_multiply_fusion, f32[384]{0:T(512)S(1)} %add_rsqrt_fusion.1, f32[2048]{0:T(1024)S(1)} %copy-done.5, f32[384]{0:T(512)S(1)} %add_rsqrt_fusion.2), kind=kLoop, calls=%fused_computation.26 | loop fusion | flops 7864320 | bytes 6304256 | tf_op jit(solution)/shard_map/convert_element_type | solution.py:419
  257.4 2.6 copy.39
  260.0 11.4 %shard_map.105 = f32[16,128]{1,0:T(8,128)} custom-call(f32[16,128]{1,0:T(8,128)} %bitcast.72), custom_call_target="tpu_custom_call" | custom-call | tf_op jit(solution)/shard_map/pallas_call | solution.py:293
  271.3 1.3 multiply_bitcast_fusion
  (75 shorter events, 2.1 us)
Async XLA Ops:
  0.6 5.0 %copy-start.7 = (s32[3]{0:T(128)S(1)}, s32[3]{0:T(128)}, u32[]{:S(2)}) copy-start(s32[3]{0:T(128)} %param.19) | copy-start | bytes 40
  0.6 5.0 %copy-start.8 = (s32[3]{0:T(128)S(1)}, s32[3]{0:T(128)}, u32[]{:S(2)}) copy-start(s32[3]{0:T(128)} %param.20) | copy-start | bytes 40
  0.7 5.0 %copy-start.6 = (f32[4096]{0:T(1024)S(1)}, f32[4096]{0:T(1024)}, u32[]{:S(2)}) copy-start(f32[4096]{0:T(1024)} %param.14) | copy-start | bytes 49156
  0.7 5.0 %copy-start.3 = (bf16[4096,256]{1,0:T(8,128)(2,1)S(1)}, bf16[4096,256]{1,0:T(8,128)(2,1)}, u32[]{:S(2)}) copy-start(bf16[4096,256]{1,0:T(8,128)(2,1)} %param.16) | copy-start | bytes 6291460
  5.6 1.9 copy-start
  169.4 3.8 %copy-start.1 = (s32[16]{0:T(128)S(1)}, s32[16]{0:T(128)}, u32[]{:S(2)}) copy-start(s32[16]{0:T(128)} %param.15) | copy-start | bytes 196
  178.2 12.3 %collective-permute-start = (bf16[2,128,256]{2,1,0:T(8,128)(2,1)S(1)}, bf16[2,128,256]{2,1,0:T(8,128)(2,1)S(1)}, u32[]{:S(2)}, u32[]{:S(2)}) collective-permute-start(bf16[2,128,256]{2,1,0:T(8,128)(2,1)S(1)} %dynamic-slice_bitcast_fusion.5), channel_id=1, source_target_pairs={{0,8},{2,10},{4,12},{6,14},{8,16},{10,18},{12,20},{14,22},{16,24},... | collective-permute-start | bytes 393224 | tf_op jit(solution)/shard_map/ppermute | solution.py:361
  181.5 9.1 %collective-permute-start.1 = (bf16[2,160,256]{2,1,0:T(8,128)(2,1)S(1)}, bf16[2,160,256]{2,1,0:T(8,128)(2,1)S(1)}, u32[]{:S(2)}, u32[]{:S(2)}) collective-permute-start(bf16[2,160,256]{2,1,0:T(8,128)(2,1)S(1)} %dynamic-slice_bitcast_fusion.4), channel_id=1, source_target_pairs={{8,0},{10,2},{12,4},{14,6},{16,8},{18,10},{20,12},{22,14},{24,16},... | collective-permute-start | bytes 491528 | tf_op jit(solution)/shard_map/ppermute | solution.py:362
  213.6 4.6 %copy-start.4 = (bf16[384,2048]{1,0:T(8,128)(2,1)S(1)}, bf16[384,2048]{1,0:T(8,128)(2,1)}, u32[]{:S(2)}) copy-start(bf16[384,2048]{1,0:T(8,128)(2,1)} %param.17) | copy-start | bytes 4718596
  214.7 12.2 %collective-permute-start.2 = (bf16[384,2,256]{2,0,1:T(8,128)(2,1)}, bf16[384,2,256]{2,0,1:T(8,128)(2,1)}, u32[]{:S(2)}, u32[]{:S(2)}) collective-permute-start(bf16[384,2,256]{2,0,1:T(8,128)(2,1)} %get-tuple-element.36), channel_id=1, source_target_pairs={{0,2},{2,0},{4,6},{6,4},{8,10},{10,8},{12,14},{14,12},{16,18},{18,... | collective-permute-start | bytes 1179656 | tf_op jit(solution)/shard_map/ppermute | solution.py:402
  216.2 19.8 %collective-permute-start.3 = (bf16[384,2,256]{2,0,1:T(8,128)(2,1)}, bf16[384,2,256]{2,0,1:T(8,128)(2,1)}, u32[]{:S(2)}, u32[]{:S(2)}) collective-permute-start(bf16[384,2,256]{2,0,1:T(8,128)(2,1)} %get-tuple-element.35), channel_id=1, source_target_pairs={{0,4},{2,6},{4,0},{6,2},{8,12},{10,14},{12,8},{14,10},{16,20},{18,... | collective-permute-start | bytes 1179656 | tf_op jit(solution)/shard_map/ppermute | solution.py:402
  216.7 19.3 %collective-permute-start.4 = (bf16[384,2,256]{2,0,1:T(8,128)(2,1)}, bf16[384,2,256]{2,0,1:T(8,128)(2,1)}, u32[]{:S(2)}, u32[]{:S(2)}) collective-permute-start(bf16[384,2,256]{2,0,1:T(8,128)(2,1)} %get-tuple-element.34), channel_id=1, source_target_pairs={{0,6},{2,4},{4,2},{6,0},{8,14},{10,12},{12,10},{14,8},{16,22},{18,... | collective-permute-start | bytes 1179656 | tf_op jit(solution)/shard_map/ppermute | solution.py:402
  219.0 19.6 %copy-start.2 = (bf16[384,2048]{0,1:T(8,128)(2,1)}, bf16[384,2048]{0,1:T(8,128)(2,1)S(1)}, u32[]{:S(2)}) copy-start(bf16[384,2048]{0,1:T(8,128)(2,1)S(1)} %copy.31) | copy-start | bytes 4718596
  243.1 4.9 %copy-start.5 = (f32[2048]{0:T(1024)S(1)}, f32[2048]{0:T(1024)}, u32[]{:S(2)}) copy-start(f32[2048]{0:T(1024)} %param.18) | copy-start | bytes 24580

commit v2 on v1

--- a/solution.py
+++ b/solution.py
@@ -34,7 +34,7 @@
     x_hbm, p_hbm, w_hbm, a_hbm,
     mapped, w_all, a_all,
     xs, ps, part, recv,
-    x_send, x_recv, u_send, d_send, p_recv, s_send, s_recv, t_send, t_recv, local,
+    x_send, x_recv, u_send, d_send, p_recv, s_send, s_recv, a_send, a_recv, t_send, t_recv, local,
 ):
     me, t = lax.axis_index("seq"), lax.axis_index("tp")
     p, q = me % g, me // g
@@ -43,21 +43,12 @@
     nl = nq // tp
 
     barrier = pltpu.get_barrier_semaphore()
-    for e in range(1, g):
-        pl.semaphore_signal(barrier, inc=1, device_id=(base + (p + e) % g, t), device_id_type=MESH)
+    n = g * nq
+    for o in range(1, n):
+        pl.semaphore_signal(barrier, inc=1, device_id=((me + o) % n, t), device_id_type=MESH)
     for o in range(1, tp):
         pl.semaphore_signal(barrier, inc=1, device_id=(me, (t + o) % tp), device_id_type=MESH)
-
-    @pl.when(q > 0)
-    def _():
-        pl.semaphore_signal(barrier, inc=1, device_id=(me - g, t), device_id_type=MESH)
-
-    @pl.when(q < nq - 1)
-    def _():
-        pl.semaphore_signal(barrier, inc=1, device_id=(me + g, t), device_id_type=MESH)
-
-    ends = (q == 0).astype(jnp.int32) + (q == nq - 1).astype(jnp.int32)
-    pl.semaphore_wait(barrier, g - 1 + tp - 1 + 2 - ends)
+    pl.semaphore_wait(barrier, n - 1 + tp - 1)
 
     def x_copy(source, e, h, member):
         return pltpu.make_async_remote_copy(
@@ -115,19 +106,24 @@
         x_copy(own(h), e, h, partner(p, e, g)[1]).start()
 
     smalls = []
-    for index, (source, target) in enumerate(((w_hbm, w_all), (a_hbm, a_all))):
-        for e in range(1, g):
-            copy = pltpu.make_async_remote_copy(
-                src_ref=source, dst_ref=target.at[p],
-                send_sem=s_send.at[index, e], recv_sem=s_recv.at[index, e],
-                device_id=(base + (p + e) % g, t), device_id_type=MESH,
-            )
-            copy.start()
-            smalls.append(copy)
+    for o in range(1, n):
+        copy = pltpu.make_async_remote_copy(
+            src_ref=a_hbm, dst_ref=a_all.at[me], send_sem=a_send.at[o], recv_sem=a_recv.at[o],
+            device_id=((me + o) % n, t), device_id_type=MESH,
+        )
+        copy.start()
+        smalls.append(copy)
+    for e in range(1, g):
+        copy = pltpu.make_async_remote_copy(
+            src_ref=w_hbm, dst_ref=w_all.at[p], send_sem=s_send.at[e], recv_sem=s_recv.at[e],
+            device_id=(base + (p + e) % g, t), device_id_type=MESH,
+        )
+        copy.start()
+        smalls.append(copy)
     locals_ = [
         pltpu.make_async_copy(p_hbm, ps.at[q], local.at[0]),
         pltpu.make_async_copy(w_hbm, w_all.at[p], local.at[1]),
-        pltpu.make_async_copy(a_hbm, a_all.at[p], local.at[2]),
+        pltpu.make_async_copy(a_hbm, a_all.at[me], local.at[2]),
     ]
     for h in range(nh):
         locals_.append(pltpu.make_async_copy(own(h), xs.at[h], local.at[3 + h]))
@@ -232,7 +228,7 @@
         out_shape=(
             jax.ShapeDtypeStruct((nl, g * nh, half, width), jnp.bfloat16),
             jax.ShapeDtypeStruct((g,) + w.shape, w.dtype),
-            jax.ShapeDtypeStruct((g,) + a.shape, a.dtype),
+            jax.ShapeDtypeStruct((g * nq,) + a.shape, a.dtype),
         ),
         in_specs=[any_spec] * 4,
         out_specs=(vmem, vmem, vmem),
@@ -246,8 +242,10 @@
             dma((nq,)),
             dma((nq,)),
             dma((nq,)),
-            dma((2, g)),
-            dma((2, g)),
+            dma((g,)),
+            dma((g,)),
+            dma((g * nq,)),
+            dma((g * nq,)),
             dma((tp,)),
             dma((tp,)),
             dma((3 + nh,)),
@@ -263,41 +261,200 @@
     )(x, p, w, a)
 
 
-def sum_kernel(n, value, total, held, send_sem, recv_sem):
+def mix_kernel(g, blocks, low, high, info, mapped, below, above, weights, mixed, held):
+    nl, width = mapped.shape[0], mapped.shape[2]
+    size = weights.shape[1]
+    live = low + mapped.shape[1] + high
+    for z in range(nl):
+        columns = slice(z * width, (z + 1) * width)
+        held[0:low, columns] = below[z]
+        held[low : live - high, columns] = mapped[z]
+        held[live - high : live, columns] = above[z]
+    held[live:, :] = jnp.zeros((held.shape[0] - live, held.shape[1]), held.dtype)
+    lanes = lax.broadcasted_iota(jnp.int32, (size, size), 1)
+
+    def one(b, carry):
+        cut = info[2 * g * blocks + b]
+        source = weights[b].astype(jnp.float32)
+        total = None
+        for part in range(2):
+            start = info[part * g * blocks + b]
+            kept = jnp.where((lanes < cut) if part == 0 else (lanes >= cut), source, 0.0)
+            spread = jnp.concatenate([kept, jnp.zeros_like(kept)], axis=1)
+            spread = pltpu.roll(spread, start % 16, axis=1).astype(jnp.bfloat16)
+            rows = held[pl.ds(pl.multiple_of(start // 16 * 16, 16), 2 * size), :]
+            product = jnp.dot(spread, rows, preferred_element_type=jnp.float32)
+            total = product if total is None else total + product
+        mixed[b] = total.astype(jnp.bfloat16)
+        return carry
+
+    lax.fori_loop(0, g * blocks, one, 0)
+
+
+def mix(g, blocks, info, mapped, below, above, weights):
+    nl, span_rows, width = mapped.shape
+    low, high, size = below.shape[1], above.shape[1], weights.shape[1]
+    vmem = pl.BlockSpec(memory_space=pltpu.VMEM)
+    return pl.pallas_call(
+        functools.partial(mix_kernel, g, blocks, low, high),
+        out_shape=jax.ShapeDtypeStruct((g * blocks, size, nl * width), jnp.bfloat16),
+        in_specs=[pl.BlockSpec(memory_space=pltpu.SMEM)] + [vmem] * 4,
+        out_specs=vmem,
+        scratch_shapes=[
+            pltpu.VMEM((low + span_rows + high + 2 * size, nl * width), jnp.bfloat16)
+        ],
+        compiler_params=pltpu.CompilerParams(vmem_limit_bytes=VMEM_LIMIT),
+    )(info, mapped, below, above, weights)
+
+
+def finish_kernel(
+    g, n, tp, nl, width, student_width, step,
+    mixed, student, gain, row_grad, gain_grad,
+    target, sums, sums_in, terms, gained, gained_in,
+    m_send, m_recv, t_send, t_recv, g_send, g_recv,
+):
     me, t = lax.axis_index("seq"), lax.axis_index("tp")
+    p = me % g
+    base = me - p
+    rows = student.shape[0]
     barrier = pltpu.get_barrier_semaphore()
     for o in range(1, n):
         pl.semaphore_signal(barrier, inc=1, device_id=((me + o) % n, t), device_id_type=MESH)
-    pl.semaphore_wait(barrier, n - 1)
+    for o in range(1, tp):
+        pl.semaphore_signal(barrier, inc=1, device_id=(me, (t + o) % tp), device_id_type=MESH)
+    pl.semaphore_wait(barrier, n - 1 + tp - 1)
+
     copies = []
+    for e in range(1, g):
+        member = partner(p, e, g)[1]
+        copy = pltpu.make_async_remote_copy(
+            src_ref=mixed.at[member], dst_ref=target.at[p],
+            send_sem=m_send.at[e], recv_sem=m_recv.at[e],
+            device_id=(base + member, t), device_id_type=MESH,
+        )
+        copy.start()
+        copies.append(copy)
+    own = pltpu.make_async_copy(mixed.at[p], target.at[p], m_send.at[0])
+    own.start()
+    own.wait()
+    for copy in copies:
+        copy.wait_recv()
+
+    tiles = [(m, z) for z in range(nl) for m in range(g)]
+
+    def load(r, m, z):
+        here = pl.ds(pl.multiple_of(r * step, step), step)
+        start = (z * g + m) * width
+        s = student[here, start : start + width].astype(jnp.float32)
+        v = target[m, here, z * width : (z + 1) * width].astype(jnp.float32)
+        return s, v, gain[:, start : start + width]
+
+    lanes = lax.broadcasted_iota(jnp.int32, (step, 128), 1)
+
+    def count(r, carry):
+        parts = [0.0] * 4
+        for m, z in tiles:
+            s, v, gn = load(r, m, z)
+            sg = s * gn
+            for k, term in enumerate((s * s, sg * sg, v * v, sg * v)):
+                parts[k] = parts[k] + term
+        packed = jnp.zeros((step, 128), jnp.float32)
+        for k in range(4):
+            packed = jnp.where(lanes == k, jnp.sum(parts[k], axis=1, keepdims=True), packed)
+        sums[pl.ds(pl.multiple_of(r * step, step), step), :] = packed
+        return carry
+
+    lax.fori_loop(0, rows // step, count, 0)
+
+    pairs = []
+    for o in range(1, tp):
+        copy = pltpu.make_async_remote_copy(
+            src_ref=sums, dst_ref=sums_in.at[o - 1],
+            send_sem=t_send.at[o - 1], recv_sem=t_recv.at[o - 1],
+            device_id=(me, (t + o) % tp), device_id_type=MESH,
+        )
+        copy.start()
+        pairs.append(copy)
+    for copy in pairs:
+        copy.wait_recv()
+
+    terms[...] = jnp.zeros_like(terms)
+
+    def grade(r, carry):
+        here = pl.ds(pl.multiple_of(r * step, step), step)
+        total = sums[here, :]
+        for o in range(1, tp):
+            total += sums_in[o - 1, here, :]
+        ss, gg, vv, sv = [total[:, k : k + 1] for k in range(4)]
+        s_scale = lax.rsqrt(ss / student_width + epsilon)
+        v_scale = lax.rsqrt(vv / student_width + epsilon)
+        inner = (s_scale * s_scale * gg - s_scale * v_scale * sv) / student_width
+        for m, z in tiles:
+            s, v, gn = load(r, m, z)
+            start = (z * g + m) * width
+            hat = s * s_scale
+            residual = hat * gn - v * v_scale
+            out = s_scale * (residual * gn - hat * inner)
+            row_grad[here, start : start + width] = out.astype(row_grad.dtype)
+            product = residual * hat
+            terms[:, start : start + width] += sum(
+                product[8 * i : 8 * i + 8] for i in range(step // 8)
+            )
+        return carry
+
+    lax.fori_loop(0, rows // step, grade, 0)
+
+    gained[...] = jnp.sum(terms[...], axis=0, keepdims=True)
+    lasts = []
     for o in range(1, n):
         copy = pltpu.make_async_remote_copy(
-            src_ref=value, dst_ref=held.at[o],
-            send_sem=send_sem.at[o], recv_sem=recv_sem.at[o],
+            src_ref=gained, dst_ref=gained_in.at[o],
+            send_sem=g_send.at[o], recv_sem=g_recv.at[o],
             device_id=((me + o) % n, t), device_id_type=MESH,
         )
         copy.start()
-        copies.append(copy)
-    acc = value[...]
-    for o, copy in zip(range(1, n), copies):
+        lasts.append(copy)
+    total = gained[...]
+    for o, copy in zip(range(1, n), lasts):
         copy.wait_recv()
-        acc += held[o]
-    total[...] = acc
-    for copy in copies:
+        total += gained_in[o]
+    gain_grad[...] = total / (rows * n)
+    for copy in copies + pairs + lasts:
         copy.wait_send()
 
 
-def sum_over_seq(n, value):
+def finish(g, n, tp, mixed, student, gain, width):
+    rows, columns = student.shape
+    nl = mixed.shape[2] // width
     vmem = pl.BlockSpec(memory_space=pltpu.VMEM)
     dma = pltpu.SemaphoreType.DMA
+    step = 32 if rows % 32 == 0 else 16
     return pl.pallas_call(
-        functools.partial(sum_kernel, n),
-        out_shape=jax.ShapeDtypeStruct(value.shape, value.dtype),
-        in_specs=[vmem],
-        out_specs=vmem,
-        scratch_shapes=[pltpu.VMEM((n,) + value.shape, value.dtype), dma((n,)), dma((n,))],
-        compiler_params=pltpu.CompilerParams(collective_id=1, has_side_effects=True),
-    )(value)
+        functools.partial(finish_kernel, g, n, tp, nl, width, columns * tp, step),
+        out_shape=(
+            jax.ShapeDtypeStruct((rows, columns), jnp.bfloat16),
+            jax.ShapeDtypeStruct((1, columns), jnp.float32),
+        ),
+        in_specs=[vmem] * 3,
+        out_specs=(vmem, vmem),
+        scratch_shapes=[
+            pltpu.VMEM(mixed.shape, mixed.dtype),
+            pltpu.VMEM((rows, 128), jnp.float32),
+            pltpu.VMEM((max(tp - 1, 1), rows, 128), jnp.float32),
+            pltpu.VMEM((8, columns), jnp.float32),
+            pltpu.VMEM((1, columns), jnp.float32),
+            pltpu.VMEM((n, 1, columns), jnp.float32),
+            dma((g,)),
+            dma((g,)),
+            dma((tp,)),
+            dma((tp,)),
+            dma((n,)),
+            dma((n,)),
+        ],
+        compiler_params=pltpu.CompilerParams(
+            collective_id=1, has_side_effects=True, vmem_limit_bytes=VMEM_LIMIT
+        ),
+    )(mixed, student, gain)
 
 
 def shards(
@@ -335,91 +492,83 @@
     aux = jnp.pad(aux, (0, aux_rows * 128 - aux.shape[0])).reshape(aux_rows, 128)
     scaled = (projector.astype(jnp.float32) * teacher_gain[:, None]).astype(jnp.bfloat16)
     mapped, weights, aux_all = gather_map(g, nq, tp, teacher_rows, scaled, align_weights, aux)
-    aux_all = aux_all.reshape(g, aux_rows * 128)
+    aux_all = aux_all.reshape(n, aux_rows * 128)
     square_sums = lax.psum(aux_all[:, :capacity], "tp")
     scales = lax.rsqrt(square_sums / teacher_width + epsilon)
-    shifts = aux_all[:, capacity : capacity + blocks].astype(jnp.int32)
-    lengths = aux_all[:, capacity + blocks : capacity + 2 * blocks].astype(jnp.int32)
+    spans = lax.dynamic_slice(aux_all, (q * g, capacity), (g, 2 * blocks)).astype(jnp.int32)
+    shifts, lengths = spans[:, :blocks], spans[:, blocks:]
 
     members = jnp.arange(g, dtype=jnp.int32)
     if g == 4:
         slot_of = jnp.bitwise_xor(members, p)
     else:
         slot_of = (p - members + g) % g
-    mapped = mapped.reshape(nl, g, capacity, width)
-    scale_slots = jnp.take(scales, slot_of, axis=0)
-    mapped = (mapped.astype(jnp.float32) * scale_slots[None, :, :, None]).astype(jnp.bfloat16)
+    mapped = mapped.reshape(nl, g * capacity, width)
 
     starts = jnp.cumsum(teacher_counts) - teacher_counts
     low = block_size
     high = 2 * block_size - (2 * rows_here - capacity) // blocks
     last_count = jnp.take(teacher_counts, q * g + g - 1)
-    tail = lax.dynamic_slice(
-        mapped, (0, slot_of[g - 1], last_count - low, 0), (nl, 1, low, width)
-    )[:, 0]
-    head = lax.dynamic_slice(mapped, (0, slot_of[0], 0, 0), (nl, 1, high, width))[:, 0]
+    tail_at = slot_of[g - 1] * capacity + last_count - low
+    tail = lax.dynamic_slice(mapped, (0, tail_at, 0), (nl, low, width))
+    head = lax.dynamic_slice(mapped, (0, slot_of[0] * capacity, 0), (nl, high, width))
     below = lax.ppermute(tail, "seq", [(i, i + g) for i in range(n - g)])
     above = lax.ppermute(head, "seq", [(i + g, i) for i in range(n - g)])
-    padded = jnp.concatenate([below, mapped.reshape(nl, g * capacity, width), above], axis=1)
 
     ids = q * g + members
-    counts = jnp.take(teacher_counts, ids)
-    own = jnp.take(starts, ids)
+    counts = lax.dynamic_slice(teacher_counts, (q * g,), (g,))
+    own = lax.dynamic_slice(starts, (q * g,), (g,))
+    after = own + counts
     block_ids = jnp.arange(blocks, dtype=jnp.int32)
     span = own[:, None] + block_ids[None, :] * counts[:, None] // blocks + shifts
     span = jnp.clip(span, 0, seq_rows - lengths)
+    before = own - jnp.concatenate([counts[:1], counts[:-1]])
+    slot_rows = low + slot_of * capacity
+    base_before = jnp.where(
+        members == 0, low - own, jnp.concatenate([slot_rows[:1], slot_rows[:-1]]) - before
+    )
+    base_own = slot_rows - own
+    base_after = (
+        jnp.where(
+            members == g - 1,
+            low + g * capacity,
+            jnp.concatenate([slot_rows[1:], slot_rows[-1:]]),
+        )
+        - after
+    )
+    is_before = span < own[:, None]
+    is_own = span < after[:, None]
+    first_base = jnp.where(
+        is_before, base_before[:, None], jnp.where(is_own, base_own[:, None], base_after[:, None])
+    )
+    second_base = jnp.where(is_before, base_own[:, None], base_after[:, None])
+    cut = jnp.where(
+        is_before, own[:, None] - span, jnp.where(is_own, after[:, None] - span, block_size)
+    )
+    cut = jnp.minimum(cut, block_size)
+    last_start = low + g * capacity + high
+    first_start = jnp.clip(span + first_base, 0, last_start)
+    second_start = jnp.clip(span + second_base, 0, last_start)
+    info = jnp.concatenate(
+        [first_start.reshape(-1), second_start.reshape(-1), cut.reshape(-1)]
+    ).astype(jnp.int32)
+
     offsets = jnp.arange(block_size, dtype=jnp.int32)
     index = span[:, :, None] + offsets
-    before = jnp.take(starts, jnp.maximum(ids - 1, 0))
-    slot_before = jnp.take(slot_of, jnp.maximum(members - 1, 0))
-    slot_after = jnp.take(slot_of, jnp.minimum(members + 1, g - 1))
-    base_before = jnp.where(members == 0, low - own, low + slot_before * capacity - before)
-    base_own = low + slot_of * capacity - own
-    base_after = jnp.where(members == g - 1, low + g * capacity, low + slot_after * capacity) - (
-        own + counts
-    )
-    wide = lambda v: v[:, None, None]
-    slot = index + jnp.where(
-        index < wide(own),
-        wide(base_before),
-        jnp.where(index < wide(own + counts), wide(base_own), wide(base_after)),
-    )
-    slot = jnp.clip(slot, 0, padded.shape[1] - 1)
-    windows = jnp.take(padded, slot.reshape(-1), axis=1).reshape(
-        nl, g * blocks, block_size, width
-    )
-    live = (offsets < lengths[:, :, None]).reshape(g * blocks, 1, block_size)
-    weights = weights.reshape(g * blocks, block_size, block_size)
-    weights = jnp.where(live, weights, jnp.zeros_like(weights))
-    mixed = jnp.einsum("bij,zbjc->bizc", weights, windows, preferred_element_type=jnp.float32)
-    mixed = mixed.astype(jnp.bfloat16).reshape(g, rows_here, nl, width)
-
-    pieces = []
-    for e in range(g):
-        piece = lax.dynamic_index_in_dim(mixed, partner(p, e, g)[1], 0, keepdims=False)
-        if e:
-            hops = [(i, i // g * g + partner(i % g, e, g)[1]) for i in range(n)]
-            piece = lax.ppermute(piece, "seq", hops)
-        pieces.append(piece)
-    target = jnp.take(jnp.stack(pieces), slot_of, axis=0)
-    target = jnp.transpose(target, (1, 2, 0, 3)).reshape(rows_here, nl * g * width)
-    target = target.astype(jnp.float32)
-
-    student = student_rows.astype(jnp.float32)
-    target_sums, student_sums = lax.psum(
-        (jnp.sum(target * target, axis=1), jnp.sum(student * student, axis=1)), "tp"
-    )
-    target_hat = target * lax.rsqrt(target_sums / student_width + epsilon)[:, None]
-    student_scale = lax.rsqrt(student_sums / student_width + epsilon)[:, None]
-    student_hat = student * student_scale
-    residual = student_hat * student_gain[None, :] - target_hat
-    weighted = residual * student_gain[None, :]
-    inner_sums = lax.psum(jnp.sum(weighted * student_hat, axis=1), "tp")
-    inner_mean = (inner_sums / student_width)[:, None]
-    row_grad = (student_scale * (weighted - student_hat * inner_mean)).astype(jnp.bfloat16)
-    gain_terms = jnp.sum(residual * student_hat, axis=0)
-    gain_grad = sum_over_seq(n, gain_terms.reshape(-1, 128)).reshape(-1) / seq_rows
-    return (row_grad, gain_grad)
+    owner = ids[:, None, None] + jnp.where(
+        index < own[:, None, None], -1, jnp.where(index < after[:, None, None], 0, 1)
+    )
+    owner = jnp.clip(owner, 0, n - 1)
+    row = jnp.clip(index - jnp.take(starts, owner), 0, capacity - 1)
+    window_scales = jnp.take(scales.reshape(-1), owner * capacity + row)
+    window_scales = jnp.where(offsets < lengths[:, :, None], window_scales, 0.0)
+    weights = weights.reshape(g * blocks, block_size, block_size).astype(jnp.float32)
+    weights = weights * window_scales.reshape(g * blocks, 1, block_size)
+    mixed = mix(g, blocks, info, mapped, below, above, weights.astype(jnp.bfloat16))
+    row_grad, gain_grad = finish(
+        g, n, tp, mixed.reshape(g, rows_here, nl * width), student_rows, student_gain[None, :], width
+    )
+    return (row_grad, gain_grad.reshape(-1))
 
 
 def solution(mesh):

time: 273 us -> 246 us (0.901)
  Pallas kernels: 171 us -> 202 us
  other arithmetic: 27.7 us -> 7.13 us
  waiting for transfers between devices: 16.6 us -> 0.01 us
  local copies, waits for them, and re-layouts: 37.8 us -> 24.2 us
  blocking collectives: 7.45 us -> 3.41 us
    pallas_call x1 -> x2, Pallas kernels: 11.4 us -> 40.1 us  [the longest x1 33.8 us: finish(): pl.pallas_call(functools.partial(finish_kernel, g, n, tp, nl, width, colu...]
    ppermute x3 -> x0, waiting for transfers between devices: 16.5 us -> none  [shards(): piece = lax.ppermute(piece, 'seq', hops)]
    concatenate x1 -> x0, local copies, waits for them, and re-layouts: 13.9 us -> none  [shards(): jnp.concatenate([below, mapped.reshape(nl, g * capacity, width), above],...]
    convert_element_type x6 -> x2, other arithmetic: 13.9 us -> 0.18 us  [the longest x1 0.1 us: shards(): weights.astype(jnp.bfloat16)]
    psum x2 -> x0, blocking collectives: 4.91 us -> none  [the longest x1 2.47 us: shards(): lax.psum((jnp.sum(target * target, axis=1), jnp.sum(student * student, ax...]
    reduce_sum x3 -> x0, other arithmetic: 4.28 us -> none  [the longest x1 3.31 us: shards(): gain_terms = jnp.sum(residual * student_hat, axis=0)]
    ppermute x3 -> x0, starting transfers between devices: 3.49 us -> none  [shards(): piece = lax.ppermute(piece, 'seq', hops)]
    gather x9 -> x3, local copies, waits for them, and re-layouts: 14 us -> 17.4 us  [the longest x2 9.05 us: shards(): row = jnp.clip(index - jnp.take(starts, owner), 0, capacity - 1)]
  transfers between devices with their start and end apart: 5 -> 2, of which waited for: 2 -> 0; matrix products, arithmetic and copies ran while one was open for 3% -> 8% of each run, Pallas kernels for 0% -> 0%
where the time goes in v2:
time: 246 us
  Pallas kernels  202 us (82%)
  local copies, waits for them, and re-layouts  24.2 us (10%)
  other arithmetic  7.13 us (3%)
  starting transfers between devices  5.86 us (2%)
  blocking collectives  3.41 us (1%)
  between operations  2.95 us (1%)
    pallas_call x1, Pallas kernels, gather_map(): pl.pallas_call(functools.partial(gather_kernel, g, nq, tp, nh), out_shape...  162 us
    pallas_call x1, Pallas kernels, finish(): pl.pallas_call(functools.partial(finish_kernel, g, n, tp, nl, width, colu...  33.8 us
    gather x2, local copies, waits for them, and re-layouts, shards(): row = jnp.clip(index - jnp.take(starts, owner), 0, capacity - 1)  9.05 us
    gather x1, local copies, waits for them, and re-layouts, shards(): window_scales = jnp.take(scales.reshape(-1), owner * capacity + row)  8.39 us
    pallas_call x1, Pallas kernels, mix(): pl.pallas_call(functools.partial(mix_kernel, g, blocks, low, high), out_s...  6.29 us
  transfers between devices with their start and end apart: 2, of which 0 were waited for; matrix products, arithmetic and copies ran while one was open for 8% of the time, Pallas kernels for 0%

profile of v2, /device:TPU:0, one launch (start us, length us, event | category | flops | bytes accessed | tf_op | source)
XLA Modules:
  0.0 245.6 jit_solution(4268604897382452784)
XLA Ops:
  0.6 0.0 copy-start.5
  0.7 0.6 fusion.12
  1.3 0.1 fusion.13
  1.4 3.0 %multiply_reduce_fusion = f32[480]{0:T(512)S(1)} fusion(bf16[480,4096]{1,0:T(8,128)(2,1)} %x_hbm.1), kind=kLoop, calls=%fused_computation.2 | loop fusion | flops 5897760 | bytes 3934080 | tf_op jit(solution)/shard_map/reduce_sum | solution.py:487
  4.4 0.1 dynamic_slice.17
  4.5 0.1 copy.12
  4.6 0.1 reduce
  4.7 0.7 compare_select_fusion.5
  5.4 0.7 fusion.9
  6.1 0.6 fusion.11
  7.4 0.0 copy-start.1
  7.4 1.7 multiply_convert_fusion.p_hbm
  9.2 0.1 fusion.7.a_hbm
  9.2 162.0 %shard_map.104 = (bf16[2,8,240,256]{3,2,1,0:T(8,128)(2,1)}, bf16[4,384,128]{2,1,0:T(8,128)(2,1)S(1)}, f32[16,8,128]{2,1,0:T(8,128)S(1)}) custom-call(bf16[480,4096]{1,0:T(8,128)(2,1)} %x_hbm.1, bf16[4096,256]{1,0:T(8,128)(2,1)} %multiply_convert_fusion.p_hbm, bf16[384,128]{1,0:T(8,128)(2,1)S(1)} %copy-done.1, f32[8,128]{1,0:T(8,128)S(1)} %fusion.7.a_hbm), custom_call_target="tpu_custom_call" | custom-call | flops 16106127360 | bytes 24117248 | tf_op jit(solution)/shard_map/pallas_call | solution.py:226
  171.3 0.9 constant_dynamic-slice_fusion
  172.2 1.3 collective-permute-start.1
  173.5 0.7 dynamic-slice.2
  175.5 1.0 constant_dynamic-slice_fusion.1
  176.5 4.6 %collective-permute-start = (bf16[2,128,256]{2,1,0:T(8,128)(2,1)S(1)}, bf16[2,128,256]{2,1,0:T(8,128)(2,1)S(1)}, u32[]{:S(2)}, u32[]{:S(2)}) collective-permute-start(bf16[2,128,256]{2,1,0:T(8,128)(2,1)S(1)} %constant_dynamic-slice_fusion.1), channel_id=1, source_target_pairs={{0,8},{2,10},{4,12},{6,14},{8,16},{10,18},{12,20},{14,22},{16,24},... | collective-permute-start | bytes 393224 | tf_op jit(solution)/shard_map/ppermute | solution.py:515
  181.1 0.1 dynamic-slice_convert_fusion
  181.2 0.1 add_clamp_fusion.3
  181.3 0.1 add.247
  181.4 0.1 compare_select_fusion.2
  181.5 9.0 %gather_fusion = s32[1536]{0:T(1024)S(1)} fusion(s32[16]{0:T(128)S(1)} %sub.67, s32[2048]{0:T(1024)S(1)} %pad_clamp_fusion.1), kind=kCustom, calls=%fused_computation | custom fusion | bytes 18432 | tf_op jit(solution)/shard_map/jit(_take)/gather | solution.py:562
  190.5 0.1 compare_select_fusion
  190.7 3.4 %psum.7 = f32[16,480]{1,0:T(8,128)S(1)} all-reduce(f32[16,480]{1,0:T(8,128)S(1)} %slice.53), channel_id=1, replica_groups=mesh['seq'=16,'tp'=2] {'tp'}, use_global_device_ids=true, to_apply=%region_2.3 | all-reduce | flops 7680 | bytes 61440 | tf_op jit(solution)/shard_map/psum | solution.py:496
  194.1 0.1 reshape.248
  194.2 0.1 lt.189
  194.3 0.1 lt.183
  194.3 0.1 lt.196
  194.4 0.1 add.230
  194.5 0.1 lt.193
  194.6 0.1 add.244
  194.7 0.1 add.245
  194.7 8.4 %gather_fusion.1 = f32[1536]{0:T(1024)S(1)} fusion(f32[7680]{0:T(1024)S(1)} %reshape.248, s32[2048]{0:T(1024)S(1)} %pad_clamp_fusion), kind=kCustom, calls=%fused_computation.1 | custom fusion | bytes 18432 | tf_op jit(solution)/shard_map/jit(_take)/gather | solution.py:563
  203.1 0.1 fusion.1
  203.2 0.1 fusion.weights
  203.3 0.1 add_clamp_fusion.2
  203.4 0.1 reshape.245
  203.5 0.1 reshape.246
  203.6 0.1 reshape.244
  203.7 0.1 pad_add_fusion.info
  203.7 0.0 collective-permute-done.below
  203.8 0.0 collective-permute-done.1.above
  203.8 6.3 %shard_map.105 = bf16[12,128,512]{2,1,0:T(8,128)(2,1)} custom-call(s32[36]{0:T(128)S(1)} %pad_add_fusion.info, bf16[2,1920,256]{2,1,0:T(8,128)(2,1)} %bitcast.46, bf16[2,128,256]{2,1,0:T(8,128)(2,1)S(1)} %collective-permute-done.below, bf16[2,160,256]{2,1,0:T(8,128)(2,1)S(1)} %collective-permute-done.1.above, bf16[12,128,128]{2,1,0:T(8,128)(2,1)S(1)} %fusion.weights), custom_call_target="tpu_custom_call" | custom-call | tf_op jit(solution)/shard_map/pallas_call | solution.py:298
  210.1 33.8 %shard_map.106 = (bf16[384,2048]{1,0:T(8,128)(2,1)S(1)}, f32[1,2048]{1,0:T(1,128)S(1)}) custom-call(bf16[4,384,512]{2,1,0:T(8,128)(2,1)} %bitcast.43, bf16[384,2048]{1,0:T(8,128)(2,1)} %student.1, f32[1,2048]{1,0:T(1,128)S(1)} %bitcast.41), custom_call_target="tpu_custom_call" | custom-call | tf_op jit(solution)/shard_map/pallas_call | solution.py:432
  243.9 1.1 copy.18
  245.0 0.6 copy.19
  (26 shorter events, 0.2 us)
Async XLA Ops:
  0.6 3.7 %copy-start.5 = (s32[3]{0:T(128)S(1)}, s32[3]{0:T(128)}, u32[]{:S(2)}) copy-start(s32[3]{0:T(128)} %param.15) | copy-start | bytes 40
  0.6 3.7 %copy-start.6 = (s32[3]{0:T(128)S(1)}, s32[3]{0:T(128)}, u32[]{:S(2)}) copy-start(s32[3]{0:T(128)} %param.16) | copy-start | bytes 40
  0.7 3.7 %copy-start.4 = (s32[16]{0:T(128)S(1)}, s32[16]{0:T(128)}, u32[]{:S(2)}) copy-start(s32[16]{0:T(128)} %param.11) | copy-start | bytes 196
  0.7 6.7 %copy-start.3 = (f32[4096]{0:T(1024)S(1)}, f32[4096]{0:T(1024)}, u32[]{:S(2)}) copy-start(f32[4096]{0:T(1024)} %param.10) | copy-start | bytes 49156
  0.7 6.7 %copy-start.2 = (bf16[4096,256]{1,0:T(8,128)(2,1)S(1)}, bf16[4096,256]{1,0:T(8,128)(2,1)}, u32[]{:S(2)}) copy-start(bf16[4096,256]{1,0:T(8,128)(2,1)} %param.12) | copy-start | bytes 6291460
  7.4 1.8 copy-start.1
  172.2 31.6 %collective-permute-start.1 = (bf16[2,160,256]{2,1,0:T(8,128)(2,1)S(1)}, bf16[2,160,256]{2,1,0:T(8,128)(2,1)S(1)}, u32[]{:S(2)}, u32[]{:S(2)}) collective-permute-start(bf16[2,160,256]{2,1,0:T(8,128)(2,1)S(1)} %constant_dynamic-slice_fusion), channel_id=1, source_target_pairs={{8,0},{10,2},{12,4},{14,6},{16,8},{18,10},{20,12},{22,14},{24,16},... | collective-permute-start | bytes 491528 | tf_op jit(solution)/shard_map/ppermute | solution.py:516
  176.5 27.3 %collective-permute-start = (bf16[2,128,256]{2,1,0:T(8,128)(2,1)S(1)}, bf16[2,128,256]{2,1,0:T(8,128)(2,1)S(1)}, u32[]{:S(2)}, u32[]{:S(2)}) collective-permute-start(bf16[2,128,256]{2,1,0:T(8,128)(2,1)S(1)} %constant_dynamic-slice_fusion.1), channel_id=1, source_target_pairs={{0,8},{2,10},{4,12},{6,14},{8,16},{10,18},{12,20},{14,22},{16,24},... | collective-permute-start | bytes 393224 | tf_op jit(solution)/shard_map/ppermute | solution.py:515
  203.7 6.3 %copy-start = (f32[2048]{0:T(1024)S(1)}, f32[2048]{0:T(1024)}, u32[]{:S(2)}) copy-start(f32[2048]{0:T(1024)} %param.14) | copy-start | bytes 24580

commit v3 on v2

--- a/solution.py
+++ b/solution.py
@@ -30,7 +30,7 @@
 
 
 def gather_kernel(
-    g, nq, tp, nh,
+    g, nq, tp, nh, np_,
     x_hbm, p_hbm, w_hbm, a_hbm,
     mapped, w_all, a_all,
     xs, ps, part, recv,
@@ -60,39 +60,46 @@
     def own(h):
         return x_hbm.at[pl.ds(h * half, half)]
 
-    def p_copy(source, block, sem, seq):
+    piece = p_hbm.shape[0] // np_
+
+    def p_copy(source, block, k, sem, seq):
         return pltpu.make_async_remote_copy(
-            src_ref=source, dst_ref=ps.at[block], send_sem=sem, recv_sem=p_recv.at[block],
+            src_ref=source, dst_ref=ps.at[block, pl.ds(k * piece, piece)],
+            send_sem=sem, recv_sem=p_recv.at[block * np_ + k],
             device_id=(seq, t), device_id_type=MESH,
         )
 
     relayed = g == 4
     direct = [1, 2] if relayed else list(range(1, g))
 
-    def up(s):
-        return p_copy(p_hbm if s == 0 else ps.at[q - s], q - s, u_send.at[s], me + g)
-
-    def down(s):
-        return p_copy(p_hbm if s == 0 else ps.at[q + s], q + s, d_send.at[s], me - g)
-
-    def forward(s):
+    def held(s, block, k):
+        here = pl.ds(k * piece, piece)
+        return p_hbm.at[here] if s == 0 else ps.at[block, here]
+
+    def up(s, k):
+        return p_copy(held(s, q - s, k), q - s, k, u_send.at[s * np_ + k], me + g)
+
+    def down(s, k):
+        return p_copy(held(s, q + s, k), q + s, k, d_send.at[s * np_ + k], me - g)
+
+    def forward(s, k):
         @pl.when(q - s >= 0)
         def _():
             if s > 0:
-                p_copy(p_hbm, q - s, u_send.at[0], me).wait_recv()
+                p_copy(held(0, q, k), q - s, k, u_send.at[0], me).wait_recv()
 
             @pl.when(q < nq - 1)
             def _():
-                up(s).start()
+                up(s, k).start()
 
         @pl.when(q + s < nq)
         def _():
             if s > 0:
-                p_copy(p_hbm, q + s, u_send.at[0], me).wait_recv()
+                p_copy(held(0, q, k), q + s, k, u_send.at[0], me).wait_recv()
 
             @pl.when(q > 0)
             def _():
-                down(s).start()
+                down(s, k).start()
 
     first = []
     for h in range(nh):
@@ -101,7 +108,8 @@
             first.append((e, k))
     for e, h in first[: len(direct)]:
         x_copy(own(h), e, h, partner(p, e, g)[1]).start()
-    forward(0)
+    for k in range(np_):
+        forward(0, k)
     for e, h in first[len(direct):]:
         x_copy(own(h), e, h, partner(p, e, g)[1]).start()
 
@@ -156,38 +164,58 @@
         def _():
             multiply(c0, c1, q + s, q + s + 1)
 
+    forward(1, 0)
     for e, h in first[: len(direct)]:
-        copy = x_copy(own(h), e, h, partner(p, e, g)[1])
-        copy.wait_recv()
+        x_copy(own(h), e, h, partner(p, e, g)[1]).wait_recv()
         if relayed:
             x_copy(xs.at[e * nh + h], 3, h, partner(p, 3 - e, g)[1]).start()
-    forward(1)
+    for k in range(1, np_):
+        forward(1, k)
+    far = nq - 1
+    for s in range(2, far):
+        forward(s, 0)
     for e, h in first[len(direct):]:
         x_copy(own(h), e, h, partner(p, e, g)[1]).wait_recv()
+    for s in range(2, far):
+        for k in range(1, np_):
+            forward(s, k)
     early = (1 + len(direct)) * nh
-    multiply(0, early, *near(1))
-    for s in range(2, nq - 1):
-        forward(s)
-        at_distance(s, 0, early)
+    multiply(0, early, *near(far - 1))
     if relayed:
         for h in range(nh):
             x_copy(xs.at[3 * nh + h], 3, h, p).wait_recv()
-        multiply(early, g * nh, *near(nq - 2))
-    forward(nq - 1)
-    at_distance(nq - 1, 0, g * nh)
-
-    sums = []
-    for o in range(1, tp):
+        multiply(early, g * nh, *near(far - 1))
+
+    def sum_copy(o, j):
         other = (t + o) % tp
-        copy = pltpu.make_async_remote_copy(
-            src_ref=part.at[pl.ds(other * nl, nl)], dst_ref=recv.at[o - 1],
-            send_sem=t_send.at[o - 1], recv_sem=t_recv.at[o - 1],
+        return pltpu.make_async_remote_copy(
+            src_ref=part.at[other * nl + j], dst_ref=recv.at[o - 1, j],
+            send_sem=t_send.at[(o - 1) * nl + j], recv_sem=t_recv.at[(o - 1) * nl + j],
             device_id=(me, other), device_id_type=MESH,
         )
-        copy.start()
-        sums.append(copy)
-    for copy in smalls + sums:
+
+    def is_far(o, j):
+        distance = (t + o) % tp * nl + j - q
+        return (distance == far) | (distance == -far)
+
+    sums = [(o, j) for o in range(1, tp) for j in range(nl)]
+    for o, j in sums:
+        @pl.when(jnp.logical_not(is_far(o, j)))
+        def _():
+            sum_copy(o, j).start()
+
+    for k in range(np_):
+        forward(far, k)
+    at_distance(far, 0, g * nh)
+    for o, j in sums:
+        @pl.when(is_far(o, j))
+        def _():
+            sum_copy(o, j).start()
+
+    for copy in smalls:
         copy.wait()
+    for o, j in sums:
+        sum_copy(o, j).wait_recv()
 
     def add(i, carry):
         block, chunk = i // (g * nh), i % (g * nh)
@@ -199,6 +227,8 @@
 
     lax.fori_loop(0, nl * g * nh, add, 0)
 
+    for o, j in sums:
+        sum_copy(o, j).wait_send()
     for e, h in first:
         x_copy(own(h), e, h, partner(p, e, g)[1]).wait_send()
     if relayed:
@@ -207,11 +237,13 @@
     for s in range(nq - 1):
         @pl.when((q - s >= 0) & (q < nq - 1))
         def _():
-            up(s).wait_send()
+            for k in range(np_):
+                up(s, k).wait_send()
 
         @pl.when((q + s < nq) & (q > 0))
         def _():
-            down(s).wait_send()
+            for k in range(np_):
+                down(s, k).wait_send()
 
 
 def gather_map(g, nq, tp, x, p, w, a):
@@ -219,12 +251,13 @@
     width = p.shape[1]
     nh = 2 if rows % 32 == 0 else 1
     half = rows // nh
+    np_ = 2
     nl = nq // tp
     any_spec = pl.BlockSpec(memory_space=pl.ANY)
     vmem = pl.BlockSpec(memory_space=pltpu.VMEM)
     dma = pltpu.SemaphoreType.DMA
     return pl.pallas_call(
-        functools.partial(gather_kernel, g, nq, tp, nh),
+        functools.partial(gather_kernel, g, nq, tp, nh, np_),
         out_shape=(
             jax.ShapeDtypeStruct((nl, g * nh, half, width), jnp.bfloat16),
             jax.ShapeDtypeStruct((g,) + w.shape, w.dtype),
@@ -239,15 +272,15 @@
             pltpu.VMEM((max(tp - 1, 1), nl, g * nh, half, width), jnp.bfloat16),
             dma((g * nh,)),
             dma((g * nh,)),
-            dma((nq,)),
-            dma((nq,)),
-            dma((nq,)),
+            dma((nq * np_,)),
+            dma((nq * np_,)),
+            dma((nq * np_,)),
             dma((g,)),
             dma((g,)),
             dma((g * nq,)),
             dma((g * nq,)),
-            dma((tp,)),
-            dma((tp,)),
+            dma((tp * nl,)),
+            dma((tp * nl,)),
             dma((3 + nh,)),
         ],
         compiler_params=pltpu.CompilerParams(
@@ -261,7 +294,7 @@
     )(x, p, w, a)
 
 
-def mix_kernel(g, blocks, low, high, info, mapped, below, above, weights, mixed, held):
+def mix_kernel(g, blocks, low, high, info, scales, mapped, below, above, weights, mixed, held):
     nl, width = mapped.shape[0], mapped.shape[2]
     size = weights.shape[1]
     live = low + mapped.shape[1] + high
@@ -274,15 +307,18 @@
     lanes = lax.broadcasted_iota(jnp.int32, (size, size), 1)
 
     def one(b, carry):
-        cut = info[2 * g * blocks + b]
-        source = weights[b].astype(jnp.float32)
+        cut, length = info[2 * g * blocks + b], info[3 * g * blocks + b]
+        source = jnp.where(lanes < length, weights[b].astype(jnp.float32), 0.0)
         total = None
         for part in range(2):
             start = info[part * g * blocks + b]
             kept = jnp.where((lanes < cut) if part == 0 else (lanes >= cut), source, 0.0)
             spread = jnp.concatenate([kept, jnp.zeros_like(kept)], axis=1)
-            spread = pltpu.roll(spread, start % 16, axis=1).astype(jnp.bfloat16)
-            rows = held[pl.ds(pl.multiple_of(start // 16 * 16, 16), 2 * size), :]
+            spread = pltpu.roll(spread, start % size, axis=1)
+            tile = start // size
+            scale = jnp.concatenate([scales[tile], scales[tile + 1]], axis=1)
+            spread = (spread * scale).astype(jnp.bfloat16)
+            rows = held[pl.ds(pl.multiple_of(tile * size, size), 2 * size), :]
             product = jnp.dot(spread, rows, preferred_element_type=jnp.float32)
             total = product if total is None else total + product
         mixed[b] = total.astype(jnp.bfloat16)
@@ -291,20 +327,20 @@
     lax.fori_loop(0, g * blocks, one, 0)
 
 
-def mix(g, blocks, info, mapped, below, above, weights):
+def mix(g, blocks, info, scales, mapped, below, above, weights):
     nl, span_rows, width = mapped.shape
     low, high, size = below.shape[1], above.shape[1], weights.shape[1]
     vmem = pl.BlockSpec(memory_space=pltpu.VMEM)
     return pl.pallas_call(
         functools.partial(mix_kernel, g, blocks, low, high),
         out_shape=jax.ShapeDtypeStruct((g * blocks, size, nl * width), jnp.bfloat16),
-        in_specs=[pl.BlockSpec(memory_space=pltpu.SMEM)] + [vmem] * 4,
+        in_specs=[pl.BlockSpec(memory_space=pltpu.SMEM)] + [vmem] * 5,
         out_specs=vmem,
         scratch_shapes=[
             pltpu.VMEM((low + span_rows + high + 2 * size, nl * width), jnp.bfloat16)
         ],
         compiler_params=pltpu.CompilerParams(vmem_limit_bytes=VMEM_LIMIT),
-    )(info, mapped, below, above, weights)
+    )(info, scales, mapped, below, above, weights)
 
 
 def finish_kernel(
@@ -549,22 +585,30 @@
     last_start = low + g * capacity + high
     first_start = jnp.clip(span + first_base, 0, last_start)
     second_start = jnp.clip(span + second_base, 0, last_start)
-    info = jnp.concatenate(
-        [first_start.reshape(-1), second_start.reshape(-1), cut.reshape(-1)]
-    ).astype(jnp.int32)
-
-    offsets = jnp.arange(block_size, dtype=jnp.int32)
-    index = span[:, :, None] + offsets
-    owner = ids[:, None, None] + jnp.where(
-        index < own[:, None, None], -1, jnp.where(index < after[:, None, None], 0, 1)
-    )
-    owner = jnp.clip(owner, 0, n - 1)
-    row = jnp.clip(index - jnp.take(starts, owner), 0, capacity - 1)
-    window_scales = jnp.take(scales.reshape(-1), owner * capacity + row)
-    window_scales = jnp.where(offsets < lengths[:, :, None], window_scales, 0.0)
-    weights = weights.reshape(g * blocks, block_size, block_size).astype(jnp.float32)
-    weights = weights * window_scales.reshape(g * blocks, 1, block_size)
-    mixed = mix(g, blocks, info, mapped, below, above, weights.astype(jnp.bfloat16))
+    info = jnp.stack(
+        [first_start, second_start, cut, lengths]
+    ).reshape(-1).astype(jnp.int32)
+
+    flat = scales.reshape(-1)
+    previous = jnp.maximum(q * g - 1, 0)
+    pieces = [
+        lax.dynamic_slice(
+            flat, (previous * capacity + jnp.take(teacher_counts, previous) - low,), (low,)
+        )
+    ]
+    for e in range(g):
+        pieces.append(
+            lax.dynamic_slice(flat, ((q * g + partner(p, e, g)[0]) * capacity,), (capacity,))
+        )
+    pieces.append(
+        lax.dynamic_slice(flat, (jnp.minimum(q * g + g, n - 1) * capacity,), (high,))
+    )
+    row_scales = jnp.concatenate(pieces)
+    tiles = -(-(last_start + 2 * block_size) // block_size)
+    row_scales = jnp.pad(row_scales, (0, tiles * block_size - row_scales.shape[0]))
+    row_scales = row_scales.reshape(tiles, 1, block_size)
+    weights = weights.reshape(g * blocks, block_size, block_size)
+    mixed = mix(g, blocks, info, row_scales, mapped, below, above, weights)
     row_grad, gain_grad = finish(
         g, n, tp, mixed.reshape(g, rows_here, nl * width), student_rows, student_gain[None, :], width
     )

time: 246 us -> 222 us (0.902)
  local copies, waits for them, and re-layouts: 24.2 us -> 7.57 us
  Pallas kernels: 202 us -> 193 us
  starting transfers between devices: 5.86 us -> 2.59 us
    gather x3 -> x0, local copies, waits for them, and re-layouts: 17.4 us -> none  [the longest x2 9.05 us: shards(): row = jnp.clip(index - jnp.take(starts, owner), 0, capacity - 1)]
    pallas_call x1, Pallas kernels: 162 us -> 154 us  [gather_map(): pl.pallas_call(functools.partial(gather_kernel, g, nq, tp, nh, np_), out_...]
    ppermute x1, starting transfers between devices: 4.57 us -> 1.3 us  [shards(): below = lax.ppermute(tail, 'seq', [(i, i + g) for i in range(n - g)])]
  transfers between devices with their start and end apart: 2 -> 2, of which waited for: 0 -> 1; matrix products, arithmetic and copies ran while one was open for 8% -> 1% of each run, Pallas kernels for 0% -> 0%
where the time goes in v3:
time: 222 us; the launch traced here: 221 us
  Pallas kernels  193 us (87%)
  other arithmetic  8.62 us (4%)
  local copies, waits for them, and re-layouts  7.57 us (3%)
  blocking collectives  4.22 us (2%)
  between operations  3.46 us (2%)
  starting transfers between devices  2.59 us (1%)
    pallas_call x1, Pallas kernels, gather_map(): pl.pallas_call(functools.partial(gather_kernel, g, nq, tp, nh, np_), out_...  154 us
    pallas_call x1, Pallas kernels, finish(): pl.pallas_call(functools.partial(finish_kernel, g, n, tp, nl, width, colu...  32.8 us
    pallas_call x1, Pallas kernels, mix(): pl.pallas_call(functools.partial(mix_kernel, g, blocks, low, high), out_s...  6.3 us
  transfers between devices with their start and end apart: 2, of which 1 were waited for; matrix products, arithmetic and copies ran while one was open for 1% of the time, Pallas kernels for 0%

profile of v3, /device:TPU:0, one launch (start us, length us, event | category | flops | bytes accessed | tf_op | source)
XLA Modules:
  0.0 221.2 jit_solution(2943619466470160321)
XLA Ops:
  0.6 0.0 copy-start.4
  0.6 0.0 copy-start.2
  0.7 0.0 copy-start.3
  0.7 0.6 fusion.7
  1.3 0.1 fusion.8
  1.3 0.7 dynamic_slice.35
  2.1 0.7 copy.12
  2.8 0.1 reduce
  3.0 0.7 sub.67
  3.6 0.7 convert_element_type.26
  4.3 0.7 convert_element_type.25
  4.9 3.0 %multiply_reduce_fusion = f32[480]{0:T(512)S(1)} fusion(bf16[480,4096]{1,0:T(8,128)(2,1)} %x_hbm.1), kind=kLoop, calls=%fused_computation | loop fusion | flops 5897760 | bytes 3934080 | tf_op jit(solution)/shard_map/reduce_sum | solution.py:523
  7.9 0.0 copy-done.4
  7.9 0.7 fusion.6
  8.6 0.7 compare_select_fusion.1
  9.3 0.7 fusion.2
  10.0 0.6 fusion.5
  12.0 0.0 copy-done.2
  12.0 0.0 copy-done.3
  12.0 0.0 copy-start.1
  12.0 1.7 multiply_convert_fusion.p_hbm
  13.7 0.1 fusion.a_hbm
  13.8 0.0 copy-done.1
  13.8 153.7 %shard_map.104 = (bf16[2,8,240,256]{3,2,1,0:T(8,128)(2,1)}, bf16[4,384,128]{2,1,0:T(8,128)(2,1)S(1)}, f32[16,8,128]{2,1,0:T(8,128)S(1)}) custom-call(bf16[480,4096]{1,0:T(8,128)(2,1)} %x_hbm.1, bf16[4096,256]{1,0:T(8,128)(2,1)} %multiply_convert_fusion.p_hbm, bf16[384,128]{1,0:T(8,128)(2,1)S(1)} %copy-done.1, f32[8,128]{1,0:T(8,128)S(1)} %fusion.a_hbm), custom_call_target="tpu_custom_call" | custom-call | flops 16106127360 | bytes 24117248 | tf_op jit(solution)/shard_map/pallas_call | solution.py:259
  167.6 1.0 constant_dynamic-slice_fusion.1
  168.5 1.3 collective-permute-start
  170.5 0.9 constant_dynamic-slice_fusion
  171.4 1.3 collective-permute-start.1
  172.7 0.1 dynamic-slice_convert_fusion
  172.8 0.1 clamp_bitcast_fusion.1
  172.9 0.1 clamp_bitcast_fusion
  173.0 4.2 %psum.7 = f32[16,480]{1,0:T(8,128)S(1)} all-reduce(f32[16,480]{1,0:T(8,128)S(1)} %slice.54), channel_id=1, replica_groups=mesh['seq'=16,'tp'=2] {'tp'}, use_global_device_ids=true, to_apply=%region_2.3 | all-reduce | flops 7680 | bytes 61440 | tf_op jit(solution)/shard_map/psum | solution.py:532
  177.3 0.1 reshape.74.info
  177.4 0.1 reshape.75
  178.1 0.1 dynamic_slice.36
  178.2 0.1 dynamic_slice.41
  178.2 0.1 fusion.4
  178.3 0.1 concatenate.19
  178.4 0.0 collective-permute-done.below
  178.4 1.9 collective-permute-done.1.above
  180.4 0.0 copy-start
  180.4 6.3 %shard_map.105 = bf16[12,128,512]{2,1,0:T(8,128)(2,1)} custom-call(s32[48]{0:T(128)S(1)} %reshape.74.info, f32[20,1,128]{2,1,0:T(1,128)S(1)} %reshape.76.scales, bf16[2,1920,256]{2,1,0:T(8,128)(2,1)} %bitcast.35, bf16[2,128,256]{2,1,0:T(8,128)(2,1)S(1)} %collective-permute-done.below, bf16[2,160,256]{2,1,0:T(8,128)(2,1)S(1)} %collective-permute-done.1.above, ...), custom_call_target="tpu_custom_call" | custom-call | tf_op jit(solution)/shard_map/pallas_call | solution.py:334
  186.7 0.0 copy-done
  186.7 32.8 %shard_map.106 = (bf16[384,2048]{1,0:T(8,128)(2,1)S(1)}, f32[1,2048]{1,0:T(1,128)S(1)}) custom-call(bf16[4,384,512]{2,1,0:T(8,128)(2,1)} %bitcast.32, bf16[384,2048]{1,0:T(8,128)(2,1)} %student.1, f32[1,2048]{1,0:T(1,128)S(1)} %bitcast.30), custom_call_target="tpu_custom_call" | custom-call | tf_op jit(solution)/shard_map/pallas_call | solution.py:468
  219.5 1.1 copy.18
  220.6 0.6 copy.19
  (8 shorter events, 0.1 us)
Async XLA Ops:
  0.6 7.3 %copy-start.4 = (s32[16]{0:T(128)S(1)}, s32[16]{0:T(128)}, u32[]{:S(2)}) copy-start(s32[16]{0:T(128)} %param.11) | copy-start | bytes 196
  0.6 11.3 %copy-start.2 = (bf16[4096,256]{1,0:T(8,128)(2,1)S(1)}, bf16[4096,256]{1,0:T(8,128)(2,1)}, u32[]{:S(2)}) copy-start(bf16[4096,256]{1,0:T(8,128)(2,1)} %param.12) | copy-start | bytes 6291460
  0.7 11.3 %copy-start.3 = (f32[4096]{0:T(1024)S(1)}, f32[4096]{0:T(1024)}, u32[]{:S(2)}) copy-start(f32[4096]{0:T(1024)} %param.10) | copy-start | bytes 49156
  12.0 1.8 copy-start.1
  168.5 9.9 %collective-permute-start = (bf16[2,128,256]{2,1,0:T(8,128)(2,1)S(1)}, bf16[2,128,256]{2,1,0:T(8,128)(2,1)S(1)}, u32[]{:S(2)}, u32[]{:S(2)}) collective-permute-start(bf16[2,128,256]{2,1,0:T(8,128)(2,1)S(1)} %constant_dynamic-slice_fusion.1), channel_id=1, source_target_pairs={{0,8},{2,10},{4,12},{6,14},{8,16},{10,18},{12,20},{14,22},{16,24},... | collective-permute-start | bytes 393224 | tf_op jit(solution)/shard_map/ppermute | solution.py:551
  171.4 8.9 %collective-permute-start.1 = (bf16[2,160,256]{2,1,0:T(8,128)(2,1)S(1)}, bf16[2,160,256]{2,1,0:T(8,128)(2,1)S(1)}, u32[]{:S(2)}, u32[]{:S(2)}) collective-permute-start(bf16[2,160,256]{2,1,0:T(8,128)(2,1)S(1)} %constant_dynamic-slice_fusion), channel_id=1, source_target_pairs={{8,0},{10,2},{12,4},{14,6},{16,8},{18,10},{20,12},{22,14},{24,16},... | collective-permute-start | bytes 491528 | tf_op jit(solution)/shard_map/ppermute | solution.py:552
  180.4 6.3 %copy-start = (f32[2048]{0:T(1024)S(1)}, f32[2048]{0:T(1024)}, u32[]{:S(2)}) copy-start(f32[2048]{0:T(1024)} %param.14) | copy-start | bytes 24580

commit v4 on v3

--- a/solution.py
+++ b/solution.py
@@ -32,9 +32,9 @@
 def gather_kernel(
     g, nq, tp, nh, np_,
     x_hbm, p_hbm, w_hbm, a_hbm,
-    mapped, w_all, a_all,
-    xs, ps, part, recv,
-    x_send, x_recv, u_send, d_send, p_recv, s_send, s_recv, a_send, a_recv, t_send, t_recv, local,
+    mapped, w_all, a_sum,
+    xs, ps, part, recv, a_all, a_in,
+    x_send, x_recv, u_send, d_send, p_recv, s_send, s_recv, a_send, a_recv, b_send, b_recv, t_send, t_recv, local,
 ):
     me, t = lax.axis_index("seq"), lax.axis_index("tp")
     p, q = me % g, me // g
@@ -139,6 +139,13 @@
         copy.start()
     for copy in locals_:
         copy.wait()
+
+    def a_copy(o):
+        return pltpu.make_async_remote_copy(
+            src_ref=a_all, dst_ref=a_in.at[o - 1],
+            send_sem=b_send.at[o - 1], recv_sem=b_recv.at[o - 1],
+            device_id=(me, (t + o) % tp), device_id_type=MESH,
+        )
 
     def multiply(c0, c1, b0, b1):
         def blocks(b, carry):
@@ -180,17 +187,16 @@
         for k in range(1, np_):
             forward(s, k)
     early = (1 + len(direct)) * nh
-    multiply(0, early, *near(far - 1))
-    if relayed:
-        for h in range(nh):
-            x_copy(xs.at[3 * nh + h], 3, h, p).wait_recv()
-        multiply(early, g * nh, *near(far - 1))
-
-    def sum_copy(o, j):
+    ranges = [(0, early), (early, g * nh)] if relayed else [(0, g * nh)]
+    nr = len(ranges)
+
+    def sum_copy(o, j, i):
         other = (t + o) % tp
+        chunks = pl.ds(ranges[i][0], ranges[i][1] - ranges[i][0])
+        sem = ((o - 1) * nl + j) * 2 + i
         return pltpu.make_async_remote_copy(
-            src_ref=part.at[other * nl + j], dst_ref=recv.at[o - 1, j],
-            send_sem=t_send.at[(o - 1) * nl + j], recv_sem=t_recv.at[(o - 1) * nl + j],
+            src_ref=part.at[other * nl + j, chunks], dst_ref=recv.at[o - 1, j, chunks],
+            send_sem=t_send.at[sem], recv_sem=t_recv.at[sem],
             device_id=(me, other), device_id_type=MESH,
         )
 
@@ -199,10 +205,21 @@
         return (distance == far) | (distance == -far)
 
     sums = [(o, j) for o in range(1, tp) for j in range(nl)]
-    for o, j in sums:
-        @pl.when(jnp.logical_not(is_far(o, j)))
-        def _():
-            sum_copy(o, j).start()
+    for i in range(nr):
+        if i == 1:
+            for h in range(nh):
+                x_copy(xs.at[3 * nh + h], 3, h, p).wait_recv()
+        multiply(*ranges[i], *near(far - 1))
+        for o, j in sums:
+            @pl.when(jnp.logical_not(is_far(o, j)))
+            def _():
+                sum_copy(o, j, i).start()
+
+        if i == 0:
+            for copy in smalls:
+                copy.wait_recv()
+            for o in range(1, tp):
+                a_copy(o).start()
 
     for k in range(np_):
         forward(far, k)
@@ -210,12 +227,17 @@
     for o, j in sums:
         @pl.when(is_far(o, j))
         def _():
-            sum_copy(o, j).start()
-
-    for copy in smalls:
-        copy.wait()
+            for i in range(nr):
+                sum_copy(o, j, i).start()
+
+    total = a_all[...]
+    for o in range(1, tp):
+        a_copy(o).wait_recv()
+        total += a_in[o - 1]
+    a_sum[...] = total
     for o, j in sums:
-        sum_copy(o, j).wait_recv()
+        for i in range(nr):
+            sum_copy(o, j, i).wait_recv()
 
     def add(i, carry):
         block, chunk = i // (g * nh), i % (g * nh)
@@ -227,8 +249,13 @@
 
     lax.fori_loop(0, nl * g * nh, add, 0)
 
+    for copy in smalls:
+        copy.wait_send()
+    for o in range(1, tp):
+        a_copy(o).wait_send()
     for o, j in sums:
-        sum_copy(o, j).wait_send()
+        for i in range(nr):
+            sum_copy(o, j, i).wait_send()
     for e, h in first:
         x_copy(own(h), e, h, partner(p, e, g)[1]).wait_send()
     if relayed:
@@ -270,6 +297,8 @@
             pltpu.VMEM((nq, depth, width), jnp.bfloat16),
             pltpu.VMEM((nq, g * nh, half, width), jnp.bfloat16),
             pltpu.VMEM((max(tp - 1, 1), nl, g * nh, half, width), jnp.bfloat16),
+            pltpu.VMEM((g * nq,) + a.shape, a.dtype),
+            pltpu.VMEM((max(tp - 1, 1), g * nq) + a.shape, a.dtype),
             dma((g * nh,)),
             dma((g * nh,)),
             dma((nq * np_,)),
@@ -279,8 +308,10 @@
             dma((g,)),
             dma((g * nq,)),
             dma((g * nq,)),
-            dma((tp * nl,)),
-            dma((tp * nl,)),
+            dma((tp,)),
+            dma((tp,)),
+            dma((2 * tp * nl,)),
+            dma((2 * tp * nl,)),
             dma((3 + nh,)),
         ],
         compiler_params=pltpu.CompilerParams(
@@ -529,9 +560,10 @@
     scaled = (projector.astype(jnp.float32) * teacher_gain[:, None]).astype(jnp.bfloat16)
     mapped, weights, aux_all = gather_map(g, nq, tp, teacher_rows, scaled, align_weights, aux)
     aux_all = aux_all.reshape(n, aux_rows * 128)
-    square_sums = lax.psum(aux_all[:, :capacity], "tp")
+    square_sums = aux_all[:, :capacity]
     scales = lax.rsqrt(square_sums / teacher_width + epsilon)
-    spans = lax.dynamic_slice(aux_all, (q * g, capacity), (g, 2 * blocks)).astype(jnp.int32)
+    spans = lax.dynamic_slice(aux_all, (q * g, capacity), (g, 2 * blocks))
+    spans = jnp.round(spans / tp).astype(jnp.int32)
     shifts, lengths = spans[:, :blocks], spans[:, blocks:]
 
     members = jnp.arange(g, dtype=jnp.int32)

time: 222 us -> 222 us (level)
  blocking collectives: 4.22 us -> 0 us
  waiting for transfers between devices: 1.91 us -> 5.99 us
    psum x1 -> x0, blocking collectives: 4.22 us -> none  [shards(): square_sums = lax.psum(aux_all[:, :capacity], 'tp')]
    ppermute x1, waiting for transfers between devices: 1.9 us -> 5.99 us  [shards(): above = lax.ppermute(head, 'seq', [(i + g, i) for i in range(n - g)])]
where the time goes in v4:
time: 222 us; the launch traced here: 221 us
  Pallas kernels  193 us (87%)
  other arithmetic  8.61 us (4%)
  local copies, waits for them, and re-layouts  7.56 us (3%)
  waiting for transfers between devices  5.99 us (3%)
  between operations  3.51 us (2%)
  starting transfers between devices  2.59 us (1%)
    pallas_call x1, Pallas kernels, gather_map(): pl.pallas_call(functools.partial(gather_kernel, g, nq, tp, nh, np_), out_...  154 us
    pallas_call x1, Pallas kernels, finish(): pl.pallas_call(functools.partial(finish_kernel, g, n, tp, nl, width, colu...  32.8 us
    pallas_call x1, Pallas kernels, mix(): pl.pallas_call(functools.partial(mix_kernel, g, blocks, low, high), out_s...  6.3 us
    ppermute x1, waiting for transfers between devices, shards(): above = lax.ppermute(head, 'seq', [(i + g, i) for i in range(n - g)])  5.99 us
  transfers between devices with their start and end apart: 2, of which 1 were waited for; matrix products, arithmetic and copies ran while one was open for 1% of the time, Pallas kernels for 0%

profile of v4, /device:TPU:0, one launch (start us, length us, event | category | flops | bytes accessed | tf_op | source)
XLA Modules:
  0.0 221.2 jit_solution(2246398265684497538)
XLA Ops:
  0.6 0.0 copy-start.4
  0.6 0.0 copy-start.2
  0.7 0.0 copy-start.3
  0.7 0.6 fusion.9
  1.3 0.1 fusion.10
  1.3 0.7 dynamic_slice.35
  2.1 0.7 copy.12
  2.8 0.1 reduce
  3.0 0.7 sub.67
  3.6 0.7 convert_element_type.26
  4.3 0.7 convert_element_type.25
  4.9 3.0 %multiply_reduce_fusion = f32[480]{0:T(512)S(1)} fusion(bf16[480,4096]{1,0:T(8,128)(2,1)} %x_hbm.1), kind=kLoop, calls=%fused_computation | loop fusion | flops 5897760 | bytes 3934080 | tf_op jit(solution)/shard_map/reduce_sum | solution.py:554
  7.9 0.0 copy-done.4
  7.9 0.7 fusion.8
  8.6 0.7 compare_select_fusion.1
  9.3 0.7 fusion.4
  10.0 0.6 fusion.7
  11.9 0.0 copy-done.2
  11.9 0.0 copy-done.3
  11.9 0.0 copy-start.1
  11.9 1.7 multiply_convert_fusion.p_hbm
  13.7 0.1 fusion.2.a_hbm
  13.7 0.0 copy-done.1
  13.7 153.9 %shard_map.104 = (bf16[2,8,240,256]{3,2,1,0:T(8,128)(2,1)}, bf16[4,384,128]{2,1,0:T(8,128)(2,1)S(1)}, f32[16,8,128]{2,1,0:T(8,128)S(1)}) custom-call(bf16[480,4096]{1,0:T(8,128)(2,1)} %x_hbm.1, bf16[4096,256]{1,0:T(8,128)(2,1)} %multiply_convert_fusion.p_hbm, bf16[384,128]{1,0:T(8,128)(2,1)S(1)} %copy-done.1, f32[8,128]{1,0:T(8,128)S(1)} %fusion.2.a_hbm), custom_call_target="tpu_custom_call" | custom-call | flops 16106127360 | bytes 24117248 | tf_op jit(solution)/shard_map/pallas_call | solution.py:286
  167.6 1.0 constant_dynamic-slice_fusion.1
  168.6 1.3 collective-permute-start
  170.5 0.9 constant_dynamic-slice_fusion
  171.4 1.3 collective-permute-start.1
  172.8 0.1 round-nearest-even_convert_fusion
  172.9 0.1 clamp_bitcast_fusion.1
  173.0 0.1 clamp_bitcast_fusion
  173.1 0.1 reshape.74.info
  173.2 0.1 reshape.75
  174.0 0.1 dynamic_slice.36
  174.1 0.1 dynamic_slice.41
  174.2 0.1 fusion.6
  174.2 0.1 concatenate.19
  174.4 0.0 collective-permute-done.below
  174.4 6.0 %collective-permute-done.1.above = bf16[2,160,256]{2,1,0:T(8,128)(2,1)S(1)} collective-permute-done((bf16[2,160,256]{2,1,0:T(8,128)(2,1)S(1)}, bf16[2,160,256]{2,1,0:T(8,128)(2,1)S(1)}, u32[]{:S(2)}, u32[]{:S(2)}) %collective-permute-start.1) | collective-permute-done | bytes 163872 | tf_op jit(solution)/shard_map/ppermute | solution.py:584
  180.4 0.0 copy-start
  180.4 6.3 %shard_map.105 = bf16[12,128,512]{2,1,0:T(8,128)(2,1)} custom-call(s32[48]{0:T(128)S(1)} %reshape.74.info, f32[20,1,128]{2,1,0:T(1,128)S(1)} %reshape.76.scales, bf16[2,1920,256]{2,1,0:T(8,128)(2,1)} %bitcast.35, bf16[2,128,256]{2,1,0:T(8,128)(2,1)S(1)} %collective-permute-done.below, bf16[2,160,256]{2,1,0:T(8,128)(2,1)S(1)} %collective-permute-done.1.above, ...), custom_call_target="tpu_custom_call" | custom-call | tf_op jit(solution)/shard_map/pallas_call | solution.py:365
  186.7 0.0 copy-done
  186.7 32.8 %shard_map.106 = (bf16[384,2048]{1,0:T(8,128)(2,1)S(1)}, f32[1,2048]{1,0:T(1,128)S(1)}) custom-call(bf16[4,384,512]{2,1,0:T(8,128)(2,1)} %bitcast.32, bf16[384,2048]{1,0:T(8,128)(2,1)} %student.1, f32[1,2048]{1,0:T(1,128)S(1)} %bitcast.30), custom_call_target="tpu_custom_call" | custom-call | tf_op jit(solution)/shard_map/pallas_call | solution.py:499
  219.4 1.1 copy.18
  220.6 0.6 copy.19
  (7 shorter events, 0.1 us)
Async XLA Ops:
  0.6 7.3 %copy-start.4 = (s32[16]{0:T(128)S(1)}, s32[16]{0:T(128)}, u32[]{:S(2)}) copy-start(s32[16]{0:T(128)} %param.11) | copy-start | bytes 196
  0.6 11.3 %copy-start.2 = (bf16[4096,256]{1,0:T(8,128)(2,1)S(1)}, bf16[4096,256]{1,0:T(8,128)(2,1)}, u32[]{:S(2)}) copy-start(bf16[4096,256]{1,0:T(8,128)(2,1)} %param.12) | copy-start | bytes 6291460
  0.7 11.3 %copy-start.3 = (f32[4096]{0:T(1024)S(1)}, f32[4096]{0:T(1024)}, u32[]{:S(2)}) copy-start(f32[4096]{0:T(1024)} %param.10) | copy-start | bytes 49156
  11.9 1.8 copy-start.1
  168.6 5.8 %collective-permute-start = (bf16[2,128,256]{2,1,0:T(8,128)(2,1)S(1)}, bf16[2,128,256]{2,1,0:T(8,128)(2,1)S(1)}, u32[]{:S(2)}, u32[]{:S(2)}) collective-permute-start(bf16[2,128,256]{2,1,0:T(8,128)(2,1)S(1)} %constant_dynamic-slice_fusion.1), channel_id=1, source_target_pairs={{0,8},{2,10},{4,12},{6,14},{8,16},{10,18},{12,20},{14,22},{16,24},... | collective-permute-start | bytes 393224 | tf_op jit(solution)/shard_map/ppermute | solution.py:583
  171.4 8.9 %collective-permute-start.1 = (bf16[2,160,256]{2,1,0:T(8,128)(2,1)S(1)}, bf16[2,160,256]{2,1,0:T(8,128)(2,1)S(1)}, u32[]{:S(2)}, u32[]{:S(2)}) collective-permute-start(bf16[2,160,256]{2,1,0:T(8,128)(2,1)S(1)} %constant_dynamic-slice_fusion), channel_id=1, source_target_pairs={{8,0},{10,2},{12,4},{14,6},{16,8},{18,10},{20,12},{22,14},{24,16},... | collective-permute-start | bytes 491528 | tf_op jit(solution)/shard_map/ppermute | solution.py:584
  180.4 6.3 %copy-start = (f32[2048]{0:T(1024)S(1)}, f32[2048]{0:T(1024)}, u32[]{:S(2)}) copy-start(f32[2048]{0:T(1024)} %param.14) | copy-start | bytes 24580

commit v5 on v4

--- a/solution.py
+++ b/solution.py
@@ -33,7 +33,7 @@
     g, nq, tp, nh, np_,
     x_hbm, p_hbm, w_hbm, a_hbm,
     mapped, w_all, a_sum,
-    xs, ps, part, recv, a_all, a_in,
+    xs, ps, part, recv, acc, a_all, a_in,
     x_send, x_recv, u_send, d_send, p_recv, s_send, s_recv, a_send, a_recv, b_send, b_recv, t_send, t_recv, local,
 ):
     me, t = lax.axis_index("seq"), lax.axis_index("tp")
@@ -161,15 +161,6 @@
 
     def near(s):
         return jnp.maximum(q - s, 0), jnp.minimum(q + s, nq - 1) + 1
-
-    def at_distance(s, c0, c1):
-        @pl.when(q - s >= 0)
-        def _():
-            multiply(c0, c1, q - s, q - s + 1)
-
-        @pl.when(q + s < nq)
-        def _():
-            multiply(c0, c1, q + s, q + s + 1)
 
     forward(1, 0)
     for e, h in first[: len(direct)]:
@@ -221,9 +212,32 @@
             for o in range(1, tp):
                 a_copy(o).start()
 
+    def last(b, k):
+        here = slice(k * piece, (k + 1) * piece)
+
+        def chunks(c, carry):
+            term = jnp.dot(xs[c, :, here], ps[b, here, :], preferred_element_type=jnp.float32)
+            if k > 0:
+                term += acc[c]
+            if k < np_ - 1:
+                acc[c] = term
+            else:
+                part[b, c] = term.astype(jnp.bfloat16)
+            return carry
+
+        lax.fori_loop(0, g * nh, chunks, 0)
+
     for k in range(np_):
         forward(far, k)
-    at_distance(far, 0, g * nh)
+
+        @pl.when(q - far >= 0)
+        def _():
+            last(q - far, k)
+
+        @pl.when(q + far < nq)
+        def _():
+            last(q + far, k)
+
     for o, j in sums:
         @pl.when(is_far(o, j))
         def _():
@@ -297,6 +311,7 @@
             pltpu.VMEM((nq, depth, width), jnp.bfloat16),
             pltpu.VMEM((nq, g * nh, half, width), jnp.bfloat16),
             pltpu.VMEM((max(tp - 1, 1), nl, g * nh, half, width), jnp.bfloat16),
+            pltpu.VMEM((g * nh, half, width), jnp.float32),
             pltpu.VMEM((g * nq,) + a.shape, a.dtype),
             pltpu.VMEM((max(tp - 1, 1), g * nq) + a.shape, a.dtype),
             dma((g * nh,)),

time: 222 us -> 223 us (level)
  no operation moved by 1% of the time
where the time goes in v5:
time: 223 us
  Pallas kernels  194 us (87%)
  other arithmetic  8.61 us (4%)
  local copies, waits for them, and re-layouts  7.56 us (3%)
  waiting for transfers between devices  5.99 us (3%)
  between operations  3.51 us (2%)
  starting transfers between devices  2.59 us (1%)
    pallas_call x1, Pallas kernels, gather_map(): pl.pallas_call(functools.partial(gather_kernel, g, nq, tp, nh, np_), out_...  155 us
    pallas_call x1, Pallas kernels, finish(): pl.pallas_call(functools.partial(finish_kernel, g, n, tp, nl, width, colu...  33.4 us
    pallas_call x1, Pallas kernels, mix(): pl.pallas_call(functools.partial(mix_kernel, g, blocks, low, high), out_s...  6.29 us
    ppermute x1, waiting for transfers between devices, shards(): above = lax.ppermute(head, 'seq', [(i + g, i) for i in range(n - g)])  5.99 us
  transfers between devices with their start and end apart: 2, of which 1 were waited for; matrix products, arithmetic and copies ran while one was open for 1% of the time, Pallas kernels for 0%

profile of v5, /device:TPU:0, one launch (start us, length us, event | category | flops | bytes accessed | tf_op | source)
XLA Modules:
  0.0 222.6 jit_solution(12759772937948047331)
XLA Ops:
  0.6 0.0 copy-start.4
  0.6 0.0 copy-start.2
  0.7 0.0 copy-start.3
  0.7 0.6 fusion.9
  1.3 0.1 fusion.10
  1.3 0.7 dynamic_slice.35
  2.1 0.7 copy.12
  2.8 0.1 reduce
  3.0 0.7 sub.67
  3.6 0.7 convert_element_type.26
  4.3 0.7 convert_element_type.25
  4.9 3.0 %multiply_reduce_fusion = f32[480]{0:T(512)S(1)} fusion(bf16[480,4096]{1,0:T(8,128)(2,1)} %x_hbm.1), kind=kLoop, calls=%fused_computation | loop fusion | flops 5897760 | bytes 3934080 | tf_op jit(solution)/shard_map/reduce_sum | solution.py:569
  7.9 0.0 copy-done.4
  7.9 0.7 fusion.8
  8.6 0.7 compare_select_fusion.1
  9.3 0.7 fusion.4
  10.0 0.6 fusion.7
  11.9 0.0 copy-done.2
  11.9 0.0 copy-done.3
  11.9 0.0 copy-start.1
  11.9 1.7 multiply_convert_fusion.p_hbm
  13.7 0.1 fusion.2.a_hbm
  13.7 0.0 copy-done.1
  13.7 154.7 %shard_map.104 = (bf16[2,8,240,256]{3,2,1,0:T(8,128)(2,1)}, bf16[4,384,128]{2,1,0:T(8,128)(2,1)S(1)}, f32[16,8,128]{2,1,0:T(8,128)S(1)}) custom-call(bf16[480,4096]{1,0:T(8,128)(2,1)} %x_hbm.1, bf16[4096,256]{1,0:T(8,128)(2,1)} %multiply_convert_fusion.p_hbm, bf16[384,128]{1,0:T(8,128)(2,1)S(1)} %copy-done.1, f32[8,128]{1,0:T(8,128)S(1)} %fusion.2.a_hbm), custom_call_target="tpu_custom_call" | custom-call | flops 16106127360 | bytes 24117248 | tf_op jit(solution)/shard_map/pallas_call | solution.py:300
  168.5 1.0 constant_dynamic-slice_fusion.1
  169.4 1.3 collective-permute-start
  171.4 0.9 constant_dynamic-slice_fusion
  172.3 1.3 collective-permute-start.1
  173.6 0.1 round-nearest-even_convert_fusion
  173.7 0.1 clamp_bitcast_fusion.1
  173.8 0.1 clamp_bitcast_fusion
  174.0 0.1 reshape.74.info
  174.1 0.1 reshape.75
  174.9 0.1 dynamic_slice.36
  175.0 0.1 dynamic_slice.41
  175.0 0.1 fusion.6
  175.1 0.1 concatenate.19
  175.2 0.0 collective-permute-done.below
  175.2 6.0 %collective-permute-done.1.above = bf16[2,160,256]{2,1,0:T(8,128)(2,1)S(1)} collective-permute-done((bf16[2,160,256]{2,1,0:T(8,128)(2,1)S(1)}, bf16[2,160,256]{2,1,0:T(8,128)(2,1)S(1)}, u32[]{:S(2)}, u32[]{:S(2)}) %collective-permute-start.1) | collective-permute-done | bytes 163872 | tf_op jit(solution)/shard_map/ppermute | solution.py:599
  181.2 0.0 copy-start
  181.2 6.3 %shard_map.105 = bf16[12,128,512]{2,1,0:T(8,128)(2,1)} custom-call(s32[48]{0:T(128)S(1)} %reshape.74.info, f32[20,1,128]{2,1,0:T(1,128)S(1)} %reshape.76.scales, bf16[2,1920,256]{2,1,0:T(8,128)(2,1)} %bitcast.35, bf16[2,128,256]{2,1,0:T(8,128)(2,1)S(1)} %collective-permute-done.below, bf16[2,160,256]{2,1,0:T(8,128)(2,1)S(1)} %collective-permute-done.1.above, ...), custom_call_target="tpu_custom_call" | custom-call | tf_op jit(solution)/shard_map/pallas_call | solution.py:380
  187.5 0.0 copy-done
  187.5 33.4 %shard_map.106 = (bf16[384,2048]{1,0:T(8,128)(2,1)S(1)}, f32[1,2048]{1,0:T(1,128)S(1)}) custom-call(bf16[4,384,512]{2,1,0:T(8,128)(2,1)} %bitcast.32, bf16[384,2048]{1,0:T(8,128)(2,1)} %student.1, f32[1,2048]{1,0:T(1,128)S(1)} %bitcast.30), custom_call_target="tpu_custom_call" | custom-call | tf_op jit(solution)/shard_map/pallas_call | solution.py:514
  220.9 1.1 copy.18
  222.0 0.6 copy.19
  (7 shorter events, 0.1 us)
Async XLA Ops:
  0.6 7.3 %copy-start.4 = (s32[16]{0:T(128)S(1)}, s32[16]{0:T(128)}, u32[]{:S(2)}) copy-start(s32[16]{0:T(128)} %param.11) | copy-start | bytes 196
  0.6 11.3 %copy-start.2 = (bf16[4096,256]{1,0:T(8,128)(2,1)S(1)}, bf16[4096,256]{1,0:T(8,128)(2,1)}, u32[]{:S(2)}) copy-start(bf16[4096,256]{1,0:T(8,128)(2,1)} %param.12) | copy-start | bytes 6291460
  0.7 11.3 %copy-start.3 = (f32[4096]{0:T(1024)S(1)}, f32[4096]{0:T(1024)}, u32[]{:S(2)}) copy-start(f32[4096]{0:T(1024)} %param.10) | copy-start | bytes 49156
  11.9 1.8 copy-start.1
  169.4 5.8 %collective-permute-start = (bf16[2,128,256]{2,1,0:T(8,128)(2,1)S(1)}, bf16[2,128,256]{2,1,0:T(8,128)(2,1)S(1)}, u32[]{:S(2)}, u32[]{:S(2)}) collective-permute-start(bf16[2,128,256]{2,1,0:T(8,128)(2,1)S(1)} %constant_dynamic-slice_fusion.1), channel_id=1, source_target_pairs={{0,8},{2,10},{4,12},{6,14},{8,16},{10,18},{12,20},{14,22},{16,24},... | collective-permute-start | bytes 393224 | tf_op jit(solution)/shard_map/ppermute | solution.py:598
  172.3 8.9 %collective-permute-start.1 = (bf16[2,160,256]{2,1,0:T(8,128)(2,1)S(1)}, bf16[2,160,256]{2,1,0:T(8,128)(2,1)S(1)}, u32[]{:S(2)}, u32[]{:S(2)}) collective-permute-start(bf16[2,160,256]{2,1,0:T(8,128)(2,1)S(1)} %constant_dynamic-slice_fusion), channel_id=1, source_target_pairs={{8,0},{10,2},{12,4},{14,6},{16,8},{18,10},{20,12},{22,14},{24,16},... | collective-permute-start | bytes 491528 | tf_op jit(solution)/shard_map/ppermute | solution.py:599
  181.2 6.3 %copy-start = (f32[2048]{0:T(1024)S(1)}, f32[2048]{0:T(1024)}, u32[]{:S(2)}) copy-start(f32[2048]{0:T(1024)} %param.14) | copy-start | bytes 24580
